TPU v7x, 32 devices: a whole 2x2x4 slice. The times are simulated.
32 devices in a mesh: section: 2 (over x), dp: 4 (over z), tensor: 4 (over y, core).
Axes of the slice: x: 2, y: 2, z: 4, core: 2. Of those that a mesh axis runs over, the one named last changes fastest.
Arguments:
- source: bfloat16 [8, 2048, 768], P('dp'), may hold values from -6 to 6
- target: bfloat16 [8, 1024, 768], P('dp'), may hold values from -6 to 6
- src_len: int32 [8], P('dp'), may hold values from 1025 to 2048, as said below
- tgt_len: int32 [8], P('dp'), may hold values from 513 to 1024, as said below
- global_mask: int32 [8, 2048], P('dp'), may hold values 0 or 1
- attn_w: bfloat16 [2, 768, 3, 768], P('section', 'dp', None, 'tensor'), may hold values from -0.21875 to 0.21875
- proj_w: bfloat16 [2, 768, 768], P('section', 'tensor', 'dp'), may hold values from -3.5 to 3.5
- cross_w: bfloat16 [2, 768, 2, 768], P('section', 'dp', None, 'tensor'), may hold values from -4 to 4
- up_w: bfloat16 [2, 768, 3072], P('section', 'dp', 'tensor'), may hold values from -0.21875 to 0.21875
- down_w: bfloat16 [2, 3072, 768], P('section', 'tensor', 'dp'), may hold values from -0.109375 to 0.109375
- norms: float32 [2, 3, 2, 768], P('section'), may hold values from -1 to 1.4
- dec_cot: bfloat16 [8, 1024, 768], P('dp'), may hold values from -6 to 6
Outputs:
- dec_out: bfloat16 [8, 1024, 768], P('dp')
- source_grad: bfloat16 [8, 2048, 768], P('dp')
- target_grad: bfloat16 [8, 1024, 768], P('dp')
- grad_attn: float32 [2, 768, 3, 768], P('section', 'dp', None, 'tensor')
- grad_proj: float32 [2, 768, 768], P('section', 'tensor', 'dp')
- grad_cross: float32 [2, 768, 2, 768], P('section', 'dp', None, 'tensor')
- grad_up: float32 [2, 768, 3072], P('section', 'dp', 'tensor')
- grad_down: float32 [2, 3072, 768], P('section', 'tensor', 'dp')
- grad_norms: float32 [2, 3, 2, 768], P('section', None, None, 'dp')
Inputs may be any that keep to these rules, and one draw needn't show every extreme that they name: `src_len`: every sequence uses more than half of its 2048 padded tokens; some sequence uses all 2048. `tgt_len`: every target uses more than half of its 1024 tokens; some target uses all 1024.
All inputs are finite; a program needn't handle non-finite values. No bound on the sum of `global_mask` on one device may be relied on, other than what follows from the above.
Results may differ from a plain program's by a relative error of at most 0.023.
Values may be sent and summed in bfloat16 or wider, within the bound.
No kernel may reach another device: no remote copies, remote signals or barrier semaphores. Data moves between devices by JAX's collectives and lax.ppermute only.
A program may use at most 512 MiB of HBM per device.

v0:
```python
import jax
import jax.numpy as jnp
from jax import lax
from jax.sharding import PartitionSpec as P

HD = 64
WINDOW = 1024


EPS = 1e-05
MASKED = -1000000000.0


def from_behind(shard, axis, by):
    devices = lax.axis_size(axis)
    pairs = [(i, i + by) for i in range(devices) if 0 <= i + by < devices]
    return lax.ppermute(shard, axis, pairs)


def gated(enabled, fn, *args):

    def skipped(*inner):
        return jax.tree.map(jnp.zeros_like, fn(*inner))

    return lax.cond(enabled, fn, skipped, *args)


def layer_norm(z, gain, shift):
    center = z - jnp.mean(z, axis=-1, keepdims=True)
    inverse = lax.rsqrt(jnp.mean(center * center, axis=-1, keepdims=True) + EPS)
    scaled = center * inverse
    return (scaled * gain + shift, (scaled, inverse))


def norm_back(grad, kept, gain):
    scaled, inverse = kept
    inner = grad * gain
    back = inverse * (
        inner
        - jnp.mean(inner, axis=-1, keepdims=True)
        - scaled * jnp.mean(inner * scaled, axis=-1, keepdims=True)
    )
    return (back, jnp.sum(grad * scaled, axis=0), jnp.sum(grad, axis=0))


def gelu_back(raised, grad):
    return jax.vjp(lambda value: jax.nn.gelu(value, approximate=False), raised)[1](grad)[0]


def head_total(partial_value):
    return lax.psum(partial_value.astype(jnp.bfloat16), "tensor").astype(jnp.float32)


def grad_total(partial_value):
    return lax.psum(partial_value.astype(jnp.bfloat16), "tensor").astype(jnp.float32)


def split_heads(matrix):
    return matrix.reshape(matrix.shape[0], matrix.shape[1] // HD, HD)


def attend_forward(query, keys, values, visible):
    count = query.shape[0]
    block = min(512, count)
    scale = HD ** (-0.5)
    query_heads = split_heads(query)
    key_heads = split_heads(keys)
    value_heads = split_heads(values)

    def one(index):
        start = index * block
        piece = lax.dynamic_slice_in_dim(query_heads, start, block, 0)
        scores = (
            jnp.einsum("qhd,khd->hqk", piece, key_heads, preferred_element_type=jnp.float32) * scale
        )
        scores = jnp.where(visible(start, block)[None], scores, MASKED)
        highest = jnp.max(scores, axis=-1, keepdims=True)
        lifted = jnp.exp(scores - highest)
        summed = jnp.sum(lifted, axis=-1, keepdims=True)
        probs = (lifted / summed).astype(jnp.bfloat16)
        context = jnp.einsum("hqk,khd->qhd", probs, value_heads, preferred_element_type=jnp.float32)
        return (context, (highest + jnp.log(summed))[..., 0])

    context, logsum = lax.map(one, jnp.arange(count // block))
    return (context.reshape(count, -1), logsum)


def attend_backward(query, keys, values, visible, logsum, grad_context):
    count = query.shape[0]
    block = min(512, count)
    scale = HD ** (-0.5)
    query_heads = split_heads(query)
    key_heads = split_heads(keys)
    value_heads = split_heads(values)
    grad_heads = split_heads(grad_context)

    def one(carry, index):
        key_sum, value_sum = carry
        start = index * block
        piece = lax.dynamic_slice_in_dim(query_heads, start, block, 0)
        grad_piece = lax.dynamic_slice_in_dim(grad_heads, start, block, 0)
        scores = (
            jnp.einsum("qhd,khd->hqk", piece, key_heads, preferred_element_type=jnp.float32) * scale
        )
        scores = jnp.where(visible(start, block)[None], scores, MASKED)
        probs = jnp.exp(scores - logsum[index][..., None])
        value_sum = value_sum + jnp.einsum(
            "hqk,qhd->khd",
            probs.astype(jnp.bfloat16),
            grad_piece,
            preferred_element_type=jnp.float32,
        )
        grad_probs = jnp.einsum(
            "qhd,khd->hqk", grad_piece, value_heads, preferred_element_type=jnp.float32
        )
        grad_scores = (
            probs * (grad_probs - jnp.sum(grad_probs * probs, axis=-1, keepdims=True))
        ).astype(jnp.bfloat16)
        grad_query = (
            jnp.einsum("hqk,khd->qhd", grad_scores, key_heads, preferred_element_type=jnp.float32)
            * scale
        )
        key_sum = (
            key_sum
            + jnp.einsum("hqk,qhd->khd", grad_scores, piece, preferred_element_type=jnp.float32)
            * scale
        )
        return ((key_sum, value_sum), grad_query)

    empty = jnp.zeros(key_heads.shape, jnp.float32)
    (grad_keys, grad_values), grad_query = lax.scan(one, (empty, empty), jnp.arange(count // block))
    return (
        grad_query.reshape(count, -1),
        grad_keys.reshape(keys.shape[0], -1),
        grad_values.reshape(values.shape[0], -1),
    )


def window_view(length, marks, count):
    place = jnp.arange(count, dtype=jnp.int32)
    marked = marks > 0

    def visible(start, block):
        queries = start + jnp.arange(block, dtype=jnp.int32)
        near = jnp.abs(queries[:, None] - place[None, :]) <= WINDOW // 2
        flagged = lax.dynamic_slice_in_dim(marked, start, block, 0)
        return (near | flagged[:, None] | marked[None, :]) & (place[None, :] < length)

    return visible


def encoder_forward(enabled, rows_in, length, marks, weights):
    attn_w, proj_w, cross_w, up_w, down_w, norms = weights
    count = rows_in.shape[0]
    valid = (jnp.arange(count, dtype=jnp.int32) < length).astype(jnp.float32)[:, None]
    visible = window_view(length, marks, count)

    def part_one(rows):
        normed, kept_zero = layer_norm(rows.astype(jnp.float32), norms[0, 0], norms[0, 1])
        normed_low = normed.astype(jnp.bfloat16)
        triple = jnp.einsum(
            "rd,dce->rce", normed_low, attn_w, preferred_element_type=jnp.float32
        ).astype(jnp.bfloat16)
        context, logsum = attend_forward(triple[:, 0], triple[:, 1], triple[:, 2], visible)
        context_low = context.astype(jnp.bfloat16)
        partial_value = jnp.dot(context_low, proj_w, preferred_element_type=jnp.float32)
        return (normed, kept_zero, normed_low, triple, logsum, context_low, partial_value)

    normed, kept_zero, normed_low, triple, logsum, context_low, partial_value = gated(
        enabled, part_one, rows_in
    )
    mixed = head_total(partial_value)

    def part_two(normed, mixed):
        middle, kept_one = layer_norm(normed + mixed, norms[1, 0], norms[1, 1])
        middle_low = middle.astype(jnp.bfloat16)
        raised = jnp.dot(middle_low, up_w, preferred_element_type=jnp.float32)
        active = jax.nn.gelu(raised, approximate=False).astype(jnp.bfloat16)
        partial_value = jnp.dot(active, down_w, preferred_element_type=jnp.float32)
        return (middle, kept_one, middle_low, raised, active, partial_value)

    middle, kept_one, middle_low, raised, active, partial_value = gated(
        enabled, part_two, normed, mixed
    )
    lowered = head_total(partial_value)

    def part_three(middle, lowered):
        memory, kept_two = layer_norm(middle + lowered, norms[2, 0], norms[2, 1])
        memory_low = (memory * valid).astype(jnp.bfloat16)
        pairs = jnp.einsum(
            "rd,dce->rce", memory_low, cross_w, preferred_element_type=jnp.float32
        ).astype(jnp.bfloat16)
        return (kept_two, memory_low, pairs)

    kept_two, memory_low, pairs = gated(enabled, part_three, middle, lowered)
    saved = (
        kept_zero,
        kept_one,
        kept_two,
        normed_low,
        triple,
        logsum,
        context_low,
        middle_low,
        raised,
        active,
        memory_low,
    )
    return (pairs, saved)


def encoder_backward(enabled, pairs_grad, saved, length, marks, weights):
    attn_w, proj_w, cross_w, up_w, down_w, norms = weights
    (
        kept_zero,
        kept_one,
        kept_two,
        normed_low,
        triple,
        logsum,
        context_low,
        middle_low,
        raised,
        active,
        memory_low,
    ) = saved
    count = normed_low.shape[0]
    valid = (jnp.arange(count, dtype=jnp.int32) < length).astype(jnp.float32)[:, None]
    visible = window_view(length, marks, count)

    def part_one(pairs_grad):
        grad_cross = jnp.einsum(
            "rd,rce->dce", memory_low, pairs_grad, preferred_element_type=jnp.float32
        )
        partial_value = jnp.einsum(
            "rce,dce->rd", pairs_grad, cross_w, preferred_element_type=jnp.float32
        )
        return (grad_cross, partial_value)

    grad_cross, partial_value = gated(enabled, part_one, pairs_grad)
    grad_memory = grad_total(partial_value) * valid

    def part_two(grad_memory):
        back_two, gain_two, shift_two = norm_back(grad_memory, kept_two, norms[2, 0])
        lowered_grad = back_two.astype(jnp.bfloat16)
        grad_down = jnp.einsum(
            "rf,rd->fd", active, lowered_grad, preferred_element_type=jnp.float32
        )
        grad_active = jnp.einsum(
            "rd,fd->rf", lowered_grad, down_w, preferred_element_type=jnp.float32
        )
        raised_grad = gelu_back(raised, grad_active).astype(jnp.bfloat16)
        grad_up = jnp.einsum(
            "rd,rf->df", middle_low, raised_grad, preferred_element_type=jnp.float32
        )
        partial_value = jnp.einsum(
            "rf,df->rd", raised_grad, up_w, preferred_element_type=jnp.float32
        )
        return (back_two, gain_two, shift_two, grad_down, grad_up, partial_value)

    back_two, gain_two, shift_two, grad_down, grad_up, partial_value = gated(
        enabled, part_two, grad_memory
    )
    grad_middle = back_two + grad_total(partial_value)

    def part_three(grad_middle):
        back_one, gain_one, shift_one = norm_back(grad_middle, kept_one, norms[1, 0])
        mixed_grad = back_one.astype(jnp.bfloat16)
        grad_proj = jnp.einsum(
            "re,rd->ed", context_low, mixed_grad, preferred_element_type=jnp.float32
        )
        context_grad = jnp.einsum(
            "rd,ed->re", mixed_grad, proj_w, preferred_element_type=jnp.float32
        ).astype(jnp.bfloat16)
        grad_query, grad_keys, grad_values = attend_backward(
            triple[:, 0], triple[:, 1], triple[:, 2], visible, logsum, context_grad
        )
        triple_grad = jnp.stack([grad_query, grad_keys, grad_values], axis=1).astype(jnp.bfloat16)
        grad_attn = jnp.einsum(
            "rd,rce->dce", normed_low, triple_grad, preferred_element_type=jnp.float32
        )
        partial_value = jnp.einsum(
            "rce,dce->rd", triple_grad, attn_w, preferred_element_type=jnp.float32
        )
        return (back_one, gain_one, shift_one, grad_proj, grad_attn, partial_value)

    back_one, gain_one, shift_one, grad_proj, grad_attn, partial_value = gated(
        enabled, part_three, grad_middle
    )
    grad_normed = back_one + grad_total(partial_value)
    back_zero, gain_zero, shift_zero = norm_back(grad_normed, kept_zero, norms[0, 0])
    grad_norms = jnp.stack(
        [
            jnp.stack([gain_zero, shift_zero]),
            jnp.stack([gain_one, shift_one]),
            jnp.stack([gain_two, shift_two]),
        ]
    )
    return (back_zero, (grad_attn, grad_proj, grad_cross, grad_up, grad_down, grad_norms))


def decoder_pass(enabled, rows_in, length, src_length, pairs, cotangent, weights):
    attn_w, proj_w, cross_w, up_w, down_w, norms = weights
    count = rows_in.shape[0]
    place = jnp.arange(count, dtype=jnp.int32)
    valid = (place < length).astype(jnp.float32)[:, None]
    memory_rows = pairs.shape[0]
    source_place = jnp.arange(memory_rows, dtype=jnp.int32)

    def causal(start, block):
        queries = start + jnp.arange(block, dtype=jnp.int32)
        return (place[None, :] <= queries[:, None]) & (place[None, :] < length)

    def reachable(start, block):
        return jnp.broadcast_to(source_place[None, :] < src_length, (block, memory_rows))

    def part_one(rows):
        triple = jnp.einsum("rd,dce->rce", rows, attn_w, preferred_element_type=jnp.float32).astype(
            jnp.bfloat16
        )
        context, logsum = attend_forward(triple[:, 0], triple[:, 1], triple[:, 2], causal)
        context_low = context.astype(jnp.bfloat16)
        partial_value = jnp.dot(context_low, proj_w, preferred_element_type=jnp.float32)
        return (triple, logsum, context_low, partial_value)

    triple, logsum, context_low, partial_value = gated(enabled, part_one, rows_in)
    mixed = head_total(partial_value)

    def part_two(mixed, pairs):
        first, kept_zero = layer_norm(rows_in.astype(jnp.float32) + mixed, norms[0, 0], norms[0, 1])
        first_low = first.astype(jnp.bfloat16)
        asking = jnp.dot(first_low, cross_w[:, 0], preferred_element_type=jnp.float32).astype(
            jnp.bfloat16
        )
        crossed, cross_logsum = attend_forward(asking, pairs[:, 0], pairs[:, 1], reachable)
        crossed_low = crossed.astype(jnp.bfloat16)
        partial_value = jnp.einsum(
            "re,de->rd", crossed_low, cross_w[:, 1], preferred_element_type=jnp.float32
        )
        return (first, kept_zero, first_low, asking, cross_logsum, crossed_low, partial_value)

    first, kept_zero, first_low, asking, cross_logsum, crossed_low, partial_value = gated(
        enabled, part_two, mixed, pairs
    )
    answer = head_total(partial_value)

    def part_three(first, answer):
        second, kept_one = layer_norm(first + answer, norms[1, 0], norms[1, 1])
        second_low = second.astype(jnp.bfloat16)
        raised = jnp.dot(second_low, up_w, preferred_element_type=jnp.float32)
        active = jax.nn.gelu(raised, approximate=False).astype(jnp.bfloat16)
        partial_value = jnp.dot(active, down_w, preferred_element_type=jnp.float32)
        return (second, kept_one, second_low, raised, active, partial_value)

    second, kept_one, second_low, raised, active, partial_value = gated(
        enabled, part_three, first, answer
    )
    lowered = head_total(partial_value)

    def part_four(second, lowered, cotangent):
        result, kept_two = layer_norm(second + lowered, norms[2, 0], norms[2, 1])
        output = (result * valid).astype(jnp.bfloat16)
        back_two, gain_two, shift_two = norm_back(
            cotangent.astype(jnp.float32) * valid, kept_two, norms[2, 0]
        )
        lowered_grad = back_two.astype(jnp.bfloat16)
        grad_down = jnp.einsum(
            "rf,rd->fd", active, lowered_grad, preferred_element_type=jnp.float32
        )
        grad_active = jnp.einsum(
            "rd,fd->rf", lowered_grad, down_w, preferred_element_type=jnp.float32
        )
        raised_grad = gelu_back(raised, grad_active).astype(jnp.bfloat16)
        grad_up = jnp.einsum(
            "rd,rf->df", second_low, raised_grad, preferred_element_type=jnp.float32
        )
        partial_value = jnp.einsum(
            "rf,df->rd", raised_grad, up_w, preferred_element_type=jnp.float32
        )
        return (output, back_two, gain_two, shift_two, grad_down, grad_up, partial_value)

    output, back_two, gain_two, shift_two, grad_down, grad_up, partial_value = gated(
        enabled, part_four, second, lowered, cotangent
    )
    grad_second = back_two + grad_total(partial_value)

    def part_five(grad_second, pairs):
        back_one, gain_one, shift_one = norm_back(grad_second, kept_one, norms[1, 0])
        answer_grad = back_one.astype(jnp.bfloat16)
        grad_output_proj = jnp.einsum(
            "rd,re->de", answer_grad, crossed_low, preferred_element_type=jnp.float32
        )
        crossed_grad = jnp.einsum(
            "rd,de->re", answer_grad, cross_w[:, 1], preferred_element_type=jnp.float32
        ).astype(jnp.bfloat16)
        asking_grad, memory_keys, memory_values = attend_backward(
            asking, pairs[:, 0], pairs[:, 1], reachable, cross_logsum, crossed_grad
        )
        asking_low = asking_grad.astype(jnp.bfloat16)
        pairs_grad = jnp.stack([memory_keys, memory_values], axis=1).astype(jnp.bfloat16)
        grad_query_proj = jnp.einsum(
            "rd,re->de", first_low, asking_low, preferred_element_type=jnp.float32
        )
        partial_value = jnp.einsum(
            "re,de->rd", asking_low, cross_w[:, 0], preferred_element_type=jnp.float32
        )
        return (
            back_one,
            gain_one,
            shift_one,
            grad_output_proj,
            grad_query_proj,
            pairs_grad,
            partial_value,
        )

    back_one, gain_one, shift_one, grad_output_proj, grad_query_proj, pairs_grad, partial_value = (
        gated(enabled, part_five, grad_second, pairs)
    )
    grad_first = back_one + grad_total(partial_value)

    def part_six(grad_first):
        back_zero, gain_zero, shift_zero = norm_back(grad_first, kept_zero, norms[0, 0])
        mixed_grad = back_zero.astype(jnp.bfloat16)
        grad_proj = jnp.einsum(
            "re,rd->ed", context_low, mixed_grad, preferred_element_type=jnp.float32
        )
        context_grad = jnp.einsum(
            "rd,ed->re", mixed_grad, proj_w, preferred_element_type=jnp.float32
        ).astype(jnp.bfloat16)
        grad_query, grad_keys, grad_values = attend_backward(
            triple[:, 0], triple[:, 1], triple[:, 2], causal, logsum, context_grad
        )
        triple_grad = jnp.stack([grad_query, grad_keys, grad_values], axis=1).astype(jnp.bfloat16)
        grad_attn = jnp.einsum(
            "rd,rce->dce", rows_in, triple_grad, preferred_element_type=jnp.float32
        )
        partial_value = jnp.einsum(
            "rce,dce->rd", triple_grad, attn_w, preferred_element_type=jnp.float32
        )
        return (back_zero, gain_zero, shift_zero, grad_proj, grad_attn, partial_value)

    back_zero, gain_zero, shift_zero, grad_proj, grad_attn, partial_value = gated(
        enabled, part_six, grad_first
    )
    grad_rows = back_zero + grad_total(partial_value)
    grad_norms = jnp.stack(
        [
            jnp.stack([gain_zero, shift_zero]),
            jnp.stack([gain_one, shift_one]),
            jnp.stack([gain_two, shift_two]),
        ]
    )
    grad_cross = jnp.stack([grad_query_proj, grad_output_proj], axis=1)
    grads = (grad_attn, grad_proj, grad_cross, grad_up, grad_down, grad_norms)
    return (output, grad_rows.astype(jnp.bfloat16), pairs_grad, grads)


def local(
    source,
    target,
    src_len,
    tgt_len,
    global_mask,
    attn_w,
    proj_w,
    cross_w,
    up_w,
    down_w,
    norms,
    dec_cot,
):
    batches = source.shape[0]
    first_section = lax.axis_index("section") == 0
    second_section = jnp.logical_not(first_section)
    gathered = (
        lax.all_gather(attn_w, "dp", axis=1, tiled=True),
        lax.all_gather(proj_w, "dp", axis=2, tiled=True),
        lax.all_gather(cross_w, "dp", axis=1, tiled=True),
        lax.all_gather(up_w, "dp", axis=1, tiled=True),
        lax.all_gather(down_w, "dp", axis=2, tiled=True),
    )
    weights = (
        gathered[0][0],
        gathered[1][0],
        gathered[2][0],
        gathered[3][0],
        gathered[4][0],
        norms[0],
    )
    pairs_out = jnp.stack(
        [
            encoder_forward(
                first_section, source[batch], src_len[batch], global_mask[batch], weights
            )[0]
            for batch in range(batches)
        ]
    )
    pairs_in = from_behind(pairs_out, "section", 1)
    outputs, row_grads, pair_grads = ([], [], [])
    dec_grads = None
    for batch in range(batches):
        output, rows_grad, pairs_grad, grads = decoder_pass(
            second_section,
            target[batch],
            tgt_len[batch],
            src_len[batch],
            pairs_in[batch],
            dec_cot[batch],
            weights,
        )
        outputs.append(output)
        row_grads.append(rows_grad)
        pair_grads.append(pairs_grad)
        dec_grads = (
            grads
            if dec_grads is None
            else tuple((left + right for left, right in zip(dec_grads, grads)))
        )
    dec_out = jnp.stack(outputs)
    target_grad = jnp.stack(row_grads)
    pairs_back = from_behind(jnp.stack(pair_grads), "section", -1)
    source_rows = []
    enc_grads = None
    for batch in range(batches):
        unused_pairs, saved = encoder_forward(
            first_section, source[batch], src_len[batch], global_mask[batch], weights
        )
        rows_grad, grads = encoder_backward(
            first_section, pairs_back[batch], saved, src_len[batch], global_mask[batch], weights
        )
        source_rows.append(rows_grad.astype(jnp.bfloat16))
        enc_grads = (
            grads
            if enc_grads is None
            else tuple((left + right for left, right in zip(enc_grads, grads)))
        )
    source_grad = jnp.stack(source_rows)
    totals = tuple((left + right for left, right in zip(dec_grads, enc_grads)))
    shares = (
        lax.psum_scatter(
            totals[0][None].astype(jnp.bfloat16), "dp", scatter_dimension=1, tiled=True
        ).astype(jnp.float32),
        lax.psum_scatter(
            totals[1][None].astype(jnp.bfloat16), "dp", scatter_dimension=2, tiled=True
        ).astype(jnp.float32),
        lax.psum_scatter(
            totals[2][None].astype(jnp.bfloat16), "dp", scatter_dimension=1, tiled=True
        ).astype(jnp.float32),
        lax.psum_scatter(
            totals[3][None].astype(jnp.bfloat16), "dp", scatter_dimension=1, tiled=True
        ).astype(jnp.float32),
        lax.psum_scatter(
            totals[4][None].astype(jnp.bfloat16), "dp", scatter_dimension=2, tiled=True
        ).astype(jnp.float32),
        lax.psum_scatter(
            totals[5][None].astype(jnp.bfloat16), "dp", scatter_dimension=3, tiled=True
        ).astype(jnp.float32),
    )
    joined = (
        lax.psum(dec_out.astype(jnp.float32).astype(jnp.bfloat16), "section").astype(jnp.float32),
        lax.psum(source_grad.astype(jnp.float32).astype(jnp.bfloat16), "section").astype(
            jnp.float32
        ),
        lax.psum(target_grad.astype(jnp.float32).astype(jnp.bfloat16), "section").astype(
            jnp.float32
        ),
    )
    return (
        joined[0].astype(jnp.bfloat16),
        joined[1].astype(jnp.bfloat16),
        joined[2].astype(jnp.bfloat16),
        shares[0],
        shares[1],
        shares[2],
        shares[3],
        shares[4],
        shares[5],
    )


def solution(mesh):
    return jax.shard_map(
        local,
        mesh=mesh,
        in_specs=(
            P("dp", None, None),
            P("dp", None, None),
            P("dp"),
            P("dp"),
            P("dp", None),
            P("section", "dp", None, "tensor"),
            P("section", "tensor", "dp"),
            P("section", "dp", None, "tensor"),
            P("section", "dp", "tensor"),
            P("section", "tensor", "dp"),
            P("section", None, None, None),
            P("dp", None, None),
        ),
        out_specs=(
            P("dp", None, None),
            P("dp", None, None),
            P("dp", None, None),
            P("section", "dp", None, "tensor"),
            P("section", "tensor", "dp"),
            P("section", "dp", None, "tensor"),
            P("section", "dp", "tensor"),
            P("section", "tensor", "dp"),
            P("section", None, None, "dp"),
        ),
        check_vma=False,
    )
```

profile of v0, /device:TPU:0, one launch (start us, length us, event | category | flops | bytes accessed | tf_op | source)
XLA Modules:
  0.0 3287.0 jit_solution(15395169194147276916)
XLA Ops:
  89.2 111.2 %conditional.31 = (f32[2048,768]{1,0:T(8,128)}, f32[2048,768]{1,0:T(8,128)}) conditional(s32[]{:T(128)} %convert_element_type.673, () %tuple.367, (bf16[2048,768]{1,0:T(8,128)(2,1)S(1)}, f32[3,2,768]{2,1,0:T(2,128)S(1)}, bf16[768,3,192]{2,1,0:T(4,128)(2,1)}, s32[2048]{0:T(1024)S(1)}, pred[2048]{0:T(1024)(128)(4,1)S(1)}, /*index=5*/s32[]{:T(128)}, ...), branch_computations={%region_7.8_spmd, %region_8.15_spmd} | conditional | flops 3266451968 | bytes 81267048 | solution.py:25
  104.9 89.7 %while.180 = (s32[]{:T(128)}, bf16[4,512,3,64]{1,3,2,0:T(8,128)(2,1)}, s32[4]{0:T(128)S(1)}, s32[2048]{0:T(1024)S(1)}, pred[2048]{0:T(1024)(128)(4,1)S(1)}, /*in...) while((s32[]{:T(128)}, ...), condition=%wide.region_14.14_spmd, body=%wide.region_11.13_spmd.sunk | while | flops 830476800 | bytes 29466832 | solution.py:84
  205.8 102.8 %conditional.34 = (f32[2048,768]{1,0:T(8,128)}, f32[2048,768]{1,0:T(8,128)}) conditional(s32[]{:T(128)} %convert_element_type.673, () %tuple.373, (bf16[2048,768]{1,0:T(8,128)(2,1)S(1)}, f32[3,2,768]{2,1,0:T(2,128)S(1)}, bf16[768,3,192]{2,1,0:T(4,128)(2,1)}, s32[2048]{0:T(1024)S(1)}, pred[2048]{0:T(1024)(128)(4,1)S(1)}, /*index=5*/s32[]{:T(128)}, ...), branch_computations={%region_25.26_spmd, %region_26.33_spmd} | conditional | flops 3266451968 | bytes 81267048 | solution.py:25
  219.6 83.1 %while.181 = (s32[]{:T(128)}, bf16[4,512,3,64]{1,3,2,0:T(8,128)(2,1)}, s32[4]{0:T(128)S(1)}, s32[2048]{0:T(1024)S(1)}, pred[2048]{0:T(1024)(128)(4,1)S(1)}, /*in...) while((s32[]{:T(128)}, ...), condition=%wide.region_32.32_spmd, body=%wide.region_29.31_spmd.sunk | while | flops 830476800 | bytes 29466832 | solution.py:84
  326.4 107.4 %all-reduce.33.cloned.1.call-done = (bf16[2048,768]{1,0:T(8,128)(2,1)}, bf16[2048,768]{1,0:T(8,128)(2,1)}) async-done(((bf16[2048,768]{1,0:T(8,128)(2,1)}, bf16[2048,768]{1,0:T(8,128)(2,1)}), (bf16[2048,768]{1,0:T(8,128)(2,1)}, bf16[2048,768]{1,0:T(8,128)(2,1)})) %all-reduce.33.cloned.1.call-update) | async-done | bytes 6291472 | tf_op jit(solution)/shard_map/psum | solution.py:51
  535.1 147.6 %all-reduce.31.cloned.1.call-done = (bf16[1024,768]{1,0:T(8,128)(2,1)}, bf16[2048,768]{1,0:T(8,128)(2,1)}, bf16[2048,768]{1,0:T(8,128)(2,1)}, bf16[1024,768]{1,0:T(8,128)(2,1)}) async-done(((bf16[1024,768]{1,0:T(8,128)(2,1)}, bf16[2048,768]{1,0:T(8,128)(2,1)}, bf16[2048,768]{1,0:T(8,128)(2,1)}, bf16[1024,768]{1,0:T(8,128)(2,1)}), (bf16[1024,768]{1,0:T(8,128)(2,1)}, bf16[2048,768]{1,0:T(8,128)(2,1)}, ...) | async-done | bytes 9437200 | tf_op jit(solution)/shard_map/psum | solution.py:51
  715.5 67.1 %collective-permute-done = bf16[2,2048,2,192]{1,3,2,0:T(8,128)(2,1)S(1)} collective-permute-done((bf16[2,2048,2,192]{1,3,2,0:T(8,128)(2,1)S(1)}, bf16[2,2048,2,192]{1,3,2,0:T(8,128)(2,1)S(1)}, u32[]{:S(2)}, u32[]{:S(2)}) %collective-permute-start) | collective-permute-done | bytes 3145760 | tf_op jit(solution)/shard_map/ppermute | solution.py:17
  809.4 144.8 %conditional.44 = (f32[2048,768]{1,0:T(8,128)}, f32[2048,768]{1,0:T(8,128)}, f32[2048,1]{0,1:T(1,128)S(1)}, bf16[2048,768]{1,0:T(8,128)(2,1)}, bf16[2048,3,192]{...) conditional(s32[]{:T(128)} %convert_element_type.673, ...), branch_computations={%region_95.96_spmd, %region_96.0_spmd} | conditional | flops 3285322752 | bytes 119293032 | solution.py:25
  838.6 107.7 %while.172 = (s32[]{:T(128)}, bf16[4,512,3,64]{1,3,2,0:T(8,128)(2,1)}, f32[4,3,512]{2,1,0:T(4,128)}, s32[4]{0:T(128)S(1)}, s32[2048]{0:T(1024)S(1)}, /*index=5*/...) while((s32[]{:T(128)}, ...), condition=%wide.region_102.102_spmd, body=%wide.region_99.101_spmd.sunk | while | flops 849347584 | bytes 47332080 | solution.py:84
  959.0 130.6 %conditional.52 = (f32[2048,768]{1,0:T(8,128)}, f32[2048,768]{1,0:T(8,128)}, f32[2048,1]{0,1:T(1,128)S(1)}, bf16[2048,768]{1,0:T(8,128)(2,1)}, bf16[2048,3,192]{...) conditional(s32[]{:T(128)} %convert_element_type.673, ...), branch_computations={%region_155.156_spmd, %region_156.163_spmd} | conditional | flops 3285322752 | bytes 122442408 | solution.py:25
  975.8 108.4 %while.173 = (s32[]{:T(128)}, bf16[4,512,3,64]{1,3,2,0:T(8,128)(2,1)}, f32[4,3,512]{2,1,0:T(4,128)}, s32[4]{0:T(128)S(1)}, s32[2048]{0:T(1024)S(1)}, /*index=5*/...) while((s32[]{:T(128)}, ...), condition=%wide.region_162.162_spmd, body=%wide.region_159.161_spmd.sunk | while | flops 849347584 | bytes 53627184 | solution.py:84
  1118.3 168.1 %all-reduce.27.cloned.1.call-done = (bf16[2048,768]{1,0:T(8,128)(2,1)}, bf16[1024,768]{1,0:T(8,128)(2,1)}, bf16[1024,768]{1,0:T(8,128)(2,1)}, bf16[2048,768]{1,0:T(8,128)(2,1)}) async-done(((bf16[2048,768]{1,0:T(8,128)(2,1)}, bf16[1024,768]{1,0:T(8,128)(2,1)}, bf16[1024,768]{1,0:T(8,128)(2,1)}, bf16[2048,768]{1,0:T(8,128)(2,1)}), (bf16[2048,768]{1,0:T(8,128)(2,1)}, bf16[1024,768]{1,0:T(8,128)(2,1)}, ...) | async-done | bytes 9437200 | tf_op jit(solution)/shard_map/psum | solution.py:51
  1402.6 169.9 %all-reduce.25.cloned.1.call-done = (bf16[2048,768]{1,0:T(8,128)(2,1)}, bf16[1024,768]{1,0:T(8,128)(2,1)}, bf16[1024,768]{1,0:T(8,128)(2,1)}, bf16[2048,768]{1,0:T(8,128)(2,1)}) async-done(((bf16[2048,768]{1,0:T(8,128)(2,1)}, bf16[1024,768]{1,0:T(8,128)(2,1)}, bf16[1024,768]{1,0:T(8,128)(2,1)}, bf16[2048,768]{1,0:T(8,128)(2,1)}), (bf16[2048,768]{1,0:T(8,128)(2,1)}, bf16[1024,768]{1,0:T(8,128)(2,1)}, ...) | async-done | bytes 9437200 | tf_op jit(solution)/shard_map/psum | solution.py:51
  1620.1 245.4 %collective-permute-done.1 = bf16[2,2048,2,192]{1,3,2,0:T(8,128)(2,1)} collective-permute-done((bf16[2,2048,2,192]{1,3,2,0:T(8,128)(2,1)}, bf16[2,2048,2,192]{1,3,2,0:T(8,128)(2,1)}, u32[]{:S(2)}, u32[]{:S(2)}) %collective-permute-start.1) | collective-permute-done | bytes 3145760 | tf_op jit(solution)/shard_map/ppermute | solution.py:17
  1891.3 112.6 %all-reduce.23.cloned.1.call-done = (bf16[2048,768]{1,0:T(8,128)(2,1)}, bf16[2048,768]{1,0:T(8,128)(2,1)}) async-done(((bf16[2048,768]{1,0:T(8,128)(2,1)}, bf16[2048,768]{1,0:T(8,128)(2,1)}), (bf16[2048,768]{1,0:T(8,128)(2,1)}, bf16[2048,768]{1,0:T(8,128)(2,1)})) %all-reduce.23.cloned.1.call-update) | async-done | bytes 6291472 | tf_op jit(solution)/shard_map/psum | solution.py:55
  2003.8 48.7 %conditional.56 = (f32[2048,768]{1,0:T(8,128)}, f32[768,768]{0,1:T(8,128)}, f32[2048,768]{1,0:T(8,128)}, f32[1,768]{1,0:T(1,128)S(1)}, f32[1,768]{1,0:T(1,128)S(1)}, /*index=5*/f32[768,768]{1,0:T(8,128)}) conditional(s32[]{:T(128)} %convert_element_type.673, () %tuple.407, (f32[2048,1]{0,1:T(1,128)}, bf16[2048,768]{1,0:T(8,128)(2,1)}, ...), branch_computations={%region_176.177_spmd, %region_177.182_spmd} | conditional | flops 9805232128 | bytes 144038096 | solution.py:25
  2059.0 47.3 %conditional.50 = (f32[2048,768]{1,0:T(8,128)}, f32[768,768]{0,1:T(8,128)}, f32[2048,768]{1,0:T(8,128)}, f32[1,768]{1,0:T(1,128)S(1)}, f32[1,768]{1,0:T(1,128)S(1)}, /*index=5*/f32[768,768]{1,0:T(8,128)}) conditional(s32[]{:T(128)} %convert_element_type.673, () %tuple.392, (f32[2048,1]{0,1:T(1,128)}, bf16[2048,768]{1,0:T(8,128)(2,1)S(1)}, ...), branch_computations={%region_136.137_spmd, %region_137.142_spmd} | conditional | flops 9805232128 | bytes 103143504 | solution.py:25
  2111.1 170.0 %all-reduce.21.cloned.1.call-done = (bf16[2048,768]{1,0:T(8,128)(2,1)}, bf16[2048,768]{1,0:T(8,128)(2,1)}, bf16[1024,768]{1,0:T(8,128)(2,1)}, bf16[1024,768]{1,0:T(8,128)(2,1)}) async-done(((bf16[2048,768]{1,0:T(8,128)(2,1)}, bf16[2048,768]{1,0:T(8,128)(2,1)}, bf16[1024,768]{1,0:T(8,128)(2,1)}, bf16[1024,768]{1,0:T(8,128)(2,1)}), (bf16[2048,768]{1,0:T(8,128)(2,1)}, bf16[2048,768]{1,0:T(8,128)(2,1)}, ...) | async-done | bytes 9437200 | tf_op jit(solution)/shard_map/psum | solution.py:55
  2303.5 227.4 %conditional.57 = (f32[2048,768]{1,0:T(8,128)}, f32[192,768]{1,0:T(8,128)}, f32[768,3,192]{0,2,1:T(8,128)}, f32[2048,768]{1,0:T(8,128)}, f32[1,768]{1,0:T(1,128)S(1)}, /*index=5*/f32[1,768]{1,0:T(1,128)S(1)}) conditional(s32[]{:T(128)} %convert_element_type.673, () %tuple.404, (f32[2048,1]{0,1:T(1,128)S(1)}, bf16[2048,768]{1,0:T(8,128)(2,1)}, ...), branch_computations={%region_183.184_spmd, %region_184.192_spmd} | conditional | flops 6934855168 | bytes 333820544 | solution.py:25
  2324.0 186.8 %while.177 = (s32[]{:T(128)}, f32[2048,3,64]{0,2,1:T(8,128)}, f32[2048,3,64]{0,2,1:T(8,128)}, bf16[4,512,3,64]{1,3,2,0:T(8,128)(2,1)}, s32[4]{0:T(128)S(1)}, /*i...) while((s32[]{:T(128)}, f32[2048,3,64]{0,2,1:T(8,128)}, ...), condition=%wide.region_189.189_spmd.clone, body=%wide.region_187.188_spmd.clone.sunk | while | flops 2068808704 | bytes 194451568 | solution.py:131
  2537.8 229.5 %conditional.51 = (f32[2048,768]{1,0:T(8,128)}, f32[192,768]{1,0:T(8,128)}, f32[768,3,192]{0,2,1:T(8,128)}, f32[2048,768]{1,0:T(8,128)}, f32[1,768]{1,0:T(1,128)}, /*index=5*/f32[1,768]{1,0:T(1,128)}) conditional(s32[]{:T(128)} %convert_element_type.673, () %tuple.389, (f32[2048,1]{0,1:T(1,128)S(1)}, bf16[2048,768]{1,0:T(8,128)(2,1)}, ...), branch_computations={%region_143.144_spmd, %region_144.152_spmd} | conditional | flops 6934855168 | bytes 302363200 | solution.py:25
  2557.5 186.6 %while.176 = (s32[]{:T(128)}, f32[2048,3,64]{0,2,1:T(8,128)}, f32[2048,3,64]{0,2,1:T(8,128)}, bf16[4,512,3,64]{1,3,2,0:T(8,128)(2,1)}, s32[4]{0:T(128)S(1)}, /*i...) while((s32[]{:T(128)}, f32[2048,3,64]{0,2,1:T(8,128)}, ...), condition=%wide.region_149.149_spmd.clone, body=%wide.region_147.148_spmd.clone.sunk | while | flops 2068808704 | bytes 194451568 | solution.py:131
  2805.5 136.6 %all-reduce.19.cloned.1.call-done = (bf16[2048,768]{1,0:T(8,128)(2,1)}, bf16[2048,768]{1,0:T(8,128)(2,1)}, bf16[1024,768]{1,0:T(8,128)(2,1)}, bf16[1024,768]{1,0:T(8,128)(2,1)}) async-done(((bf16[2048,768]{1,0:T(8,128)(2,1)}, bf16[2048,768]{1,0:T(8,128)(2,1)}, bf16[1024,768]{1,0:T(8,128)(2,1)}, bf16[1024,768]{1,0:T(8,128)(2,1)}), (bf16[2048,768]{1,0:T(8,128)(2,1)}, bf16[2048,768]{1,0:T(8,128)(2,1)}, ...) | async-done | bytes 9437200 | tf_op jit(solution)/shard_map/psum | solution.py:55
  2990.8 278.1 %all-reduce.35.cloned.1.call-done = (bf16[2,1024,768]{2,1,0:T(8,128)(2,1)}, bf16[2,2048,768]{2,1,0:T(8,128)(2,1)}, bf16[2,1024,768]{2,1,0:T(8,128)(2,1)}) async-done(((bf16[2,1024,768]{2,1,0:T(8,128)(2,1)}, bf16[2,2048,768]{2,1,0:T(8,128)(2,1)}, bf16[2,1024,768]{2,1,0:T(8,128)(2,1)}), (bf16[2,1024,768]{2,1,0:T(8,128)(2,1)}, bf16[2,2048,768]{2,1,0:T(8,128)(2,1)}, ...) | async-done | bytes 12582928 | tf_op jit(solution)/shard_map/psum | solution.py:561
  (1218 shorter events, 1908.4 us)
Async XLA Ops:
  8.0 318.3 %all-gather.3.cloned.1.call-start = ((), (), s32[]{:S(2)}) async-start(), calls=%async_computation.6 | async-start | bytes 1474560 | tf_op jit(solution)/shard_map/all_gather | solution.py:480
  8.8 317.6 %all-gather.5.cloned.1.call-start = ((), (), s32[]{:S(2)}) async-start(), calls=%async_computation.7 | async-start | bytes 1474560 | tf_op jit(solution)/shard_map/all_gather | solution.py:481
  9.5 424.2 %all-reduce.33.cloned.1.call-start = ((), (), s32[]{:S(2)}) async-start(), calls=%async_computation.21 | async-start | bytes 12582912 | tf_op jit(solution)/shard_map/psum | solution.py:51
  40.5 280.4 %copy-start.51 = (bf16[1,192,768]{2,1,0:T(8,128)(2,1)}, bf16[1,192,768]{2,1,0:T(8,128)(2,1)S(1)}, u32[]{:S(2)}) copy-start(bf16[1,192,768]{2,1,0:T(8,128)(2,1)S(1)} %copy.314) | copy-start | bytes 884740
  313.3 369.4 %all-reduce.31.cloned.1.call-start = ((), (), s32[]{:S(2)}) async-start(), calls=%async_computation.20 | async-start | bytes 18874368 | tf_op jit(solution)/shard_map/psum | solution.py:51
  512.6 584.6 %all-reduce.29.cloned.1.call-start = ((), (), s32[]{:S(2)}) async-start(), calls=%async_computation.19 | async-start | bytes 6291456 | tf_op jit(solution)/shard_map/psum | solution.py:51
  533.2 251.5 %copy-start.47 = (bf16[1,768,2,192]{3,2,0,1:T(2,128)(2,1)}, bf16[1,768,2,192]{3,2,0,1:T(2,128)(2,1)S(1)}, u32[]{:S(2)}) copy-start(bf16[1,768,2,192]{3,2,0,1:T(2,128)(2,1)S(1)} %all_gather.17) | copy-start | bytes 1769476
  713.9 68.7 %collective-permute-start = (bf16[2,2048,2,192]{1,3,2,0:T(8,128)(2,1)S(1)}, bf16[2,2048,2,192]{1,3,2,0:T(8,128)(2,1)S(1)}, u32[]{:S(2)}, u32[]{:S(2)}) collective-permute-start(bf16[2,2048,2,192]{1,3,2,0:T(8,128)(2,1)S(1)} %pad_maximum_fusion.15), channel_id=1, source_target_pairs={{0,16},{1,17},{2,18},{3,19},{4,20},{5,21},{6,22},{7,23},{8,24},{9,... | collective-permute-start | bytes 9437192 | tf_op jit(solution)/shard_map/ppermute | solution.py:17
  809.3 477.1 %all-reduce.27.cloned.1.call-start = ((), (), s32[]{:S(2)}) async-start(), calls=%async_computation.18 | async-start | bytes 18874368 | tf_op jit(solution)/shard_map/psum | solution.py:51
  1115.9 456.7 %all-reduce.25.cloned.1.call-start = ((), (), s32[]{:S(2)}) async-start(), calls=%async_computation.17 | async-start | bytes 18874368 | tf_op jit(solution)/shard_map/psum | solution.py:51
  1402.6 601.3 %all-reduce.23.cloned.1.call-start = ((), (), s32[]{:S(2)}) async-start(), calls=%async_computation.16 | async-start | bytes 12582912 | tf_op jit(solution)/shard_map/psum | solution.py:55
  1593.6 271.8 %collective-permute-start.1 = (bf16[2,2048,2,192]{1,3,2,0:T(8,128)(2,1)}, bf16[2,2048,2,192]{1,3,2,0:T(8,128)(2,1)}, u32[]{:S(2)}, u32[]{:S(2)}) collective-permute-start(bf16[2,2048,2,192]{1,3,2,0:T(8,128)(2,1)} %pad_maximum_fusion.17), channel_id=1, source_target_pairs={{16,0},{17,1},{18,2},{19,3},{20,4},{21,5},{22,6},{23,7},{24,8},{25... | collective-permute-start | bytes 9437192 | tf_op jit(solution)/shard_map/ppermute | solution.py:17
  1604.0 261.5 %copy-start.48 = (bf16[1,768,2,192]{3,2,0,1:T(2,128)(2,1)S(1)}, bf16[1,768,2,192]{3,2,0,1:T(2,128)(2,1)}, u32[]{:S(2)}) copy-start(bf16[1,768,2,192]{3,2,0,1:T(2,128)(2,1)} %copy-done.47) | copy-start | bytes 1769476
  1620.0 245.4 %copy-start.132 = (bf16[2048,768]{1,0:T(8,128)(2,1)}, bf16[2048,768]{1,0:T(8,128)(2,1)S(1)}, u32[]{:S(2)}) copy-start(bf16[2048,768]{1,0:T(8,128)(2,1)S(1)} %get-tuple-element.1802) | copy-start | bytes 9437188
  1620.0 245.4 %copy-start.40 = (f32[2048,768]{1,0:T(8,128)}, f32[2048,768]{1,0:T(8,128)S(1)}, u32[]{:S(2)}) copy-start(f32[2048,768]{1,0:T(8,128)S(1)} %get-tuple-element.1804) | copy-start | bytes 18874372
  1884.6 396.5 %all-reduce.21.cloned.1.call-start = ((), (), s32[]{:S(2)}) async-start(), calls=%async_computation.15 | async-start | bytes 18874368 | tf_op jit(solution)/shard_map/psum | solution.py:55
  2111.1 831.1 %all-reduce.19.cloned.1.call-start = ((), (), s32[]{:S(2)}) async-start(), calls=%async_computation.14 | async-start | bytes 18874368 | tf_op jit(solution)/shard_map/psum | solution.py:55
  2772.1 207.2 %reduce-scatter.23.cloned.1.call-start = ((), (), s32[]{:S(2)}) async-start(), calls=%async_computation.12 | async-start | bytes 737280
  2777.5 203.8 %reduce-scatter.17.cloned.1.call-start = ((), (), s32[]{:S(2)}) async-start(), calls=%async_computation.9 | async-start | bytes 1474560 | tf_op jit(solution)/shard_map/reduce_scatter | solution.py:553
  2782.9 200.2 %reduce-scatter.15.cloned.1.call-start = ((), (), s32[]{:S(2)}) async-start(), calls=%async_computation.8 | async-start | bytes 1474560 | tf_op jit(solution)/shard_map/reduce_scatter | solution.py:550
  2788.3 196.5 %reduce-scatter.21.cloned.1.call-start = ((), (), s32[]{:S(2)}) async-start(), calls=%async_computation.11 | async-start | bytes 491520
  2796.4 190.4 %reduce-scatter.19.cloned.1.call-start = ((), (), s32[]{:S(2)}) async-start(), calls=%async_computation.10 | async-start | bytes 1228800
  2804.0 185.1 %reduce-scatter.25.cloned.1.call-start = ((), (), s32[]{:S(2)}) async-start(), calls=%async_computation.13 | async-start | bytes 245760
  2958.2 310.8 %all-reduce.35.cloned.1.call-start = ((), (), s32[]{:S(2)}) async-start(), calls=%async_computation.22 | async-start | bytes 25165824 | tf_op jit(solution)/shard_map/psum | solution.py:561
  (271 other events, 3330.0 us)
Sparse Core Ops, SparseCore 0:
  10.4 46.7 all-gather.2
  58.8 35.5 all-gather.4
  2777.6 21.1 reduce-scatter.22
  2801.0 27.5 reduce-scatter.16
  2830.7 27.8 reduce-scatter.14
  2861.4 19.2 reduce-scatter.20
  2883.1 24.3 reduce-scatter.18
  2958.3 19.5 reduce-scatter.24
  2981.3 287.6 all-reduce.34
Sparse Core Ops, SparseCore 1:
  313.4 120.2 all-reduce.32
  512.7 169.9 all-reduce.30
  809.4 134.9 all-reduce.28
  1115.9 170.5 all-reduce.26
  1402.6 169.9 all-reduce.24
  1884.7 119.1 all-reduce.22
  2111.2 169.9 all-reduce.20
  2772.2 169.9 all-reduce.18
where the time goes:
time: 3300 us; the launch traced here: 3290 us
  waiting for transfers between devices  1600 us (48%)
  matrix products  766 us (23%)
  other arithmetic  492 us (15%)
  local copies, waits for them, and re-layouts  257 us (8%)
  blocking collectives  90.8 us (3%)
  loops' own time  56 us (2%)
    psum x5, waiting for transfers between devices, head_total(): lax.psum(partial_value.astype(jnp.bfloat16), 'tensor').astype(jnp.float32)  593 us
    psum x3, waiting for transfers between devices, grad_total(): lax.psum(partial_value.astype(jnp.bfloat16), 'tensor').astype(jnp.float32)  419 us
    ppermute x2, waiting for transfers between devices, from_behind(): return lax.ppermute(shard, axis, pairs)  313 us
    psum x1, waiting for transfers between devices, local(): lax.psum(dec_out.astype(jnp.float32).astype(jnp.bfloat16), 'section')  278 us
    dot_general x16, matrix products, one(): jnp.einsum('qhd,khd->hqk', piece, key_heads, preferred_element_type=jnp.f...  118 us
    dot_general x16, matrix products, one(): jnp.einsum('hqk,khd->qhd', probs, value_heads, preferred_element_type=jnp...  116 us
    another operation x66, local copies, waits for them, and re-layouts  85.2 us
    sub x8, matrix products, one(): lifted = jnp.exp(scores - highest)  80.4 us
  transfers between devices with their start and end apart: 19, of which 10 were waited for; matrix products, arithmetic and copies ran while one was open for 19% of the time, Pallas kernels for 0%

commit v1 on v0

v1 whole, which is shorter than its diff:
```python
import jax
import jax.numpy as jnp
from jax import lax
from jax.experimental import pallas as pl
from jax.experimental.pallas import tpu as pltpu
from jax.sharding import Mesh, PartitionSpec as P

HD = 64
WINDOW = 1024
EPS = 1e-05
MASKED = -1000000000.0
BF = jnp.bfloat16
F32 = jnp.float32
GROUP = 256
EVERY = ("section", "ty", "tc", "dp")


def dot(a, b, ca, cb):
    return lax.dot_general(a, b, (((ca,), (cb,)), ((), ())), preferred_element_type=F32)


def swap(value, axis):
    return lax.ppermute(value, axis, [(0, 1), (1, 0)])


def attend_forward_kernel(q_ref, ko_ref, kp_ref, vo_ref, vp_ref, bias_ref, ctx_ref, wide_ref, lse_ref):
    half = ko_ref.shape[1]
    step = 256
    ones = jnp.ones((16, step), BF)
    for head in range(q_ref.shape[0] // HD):
        feats = pl.ds(head * HD, HD)
        query = q_ref[feats, :]
        pieces = []
        highest = None
        for k_ref, v_ref, base in ((ko_ref, vo_ref, 0), (kp_ref, vp_ref, half)):
            for at in range(0, half, step):
                keys = pl.ds(at, step)
                scores = dot(k_ref[feats, keys], query, 0, 0) + bias_ref[pl.ds(base + at, step), :]
                top = jnp.max(scores, axis=0, keepdims=True)
                highest = top if highest is None else jnp.maximum(highest, top)
                pieces.append((scores, v_ref, keys))
        total = None
        summed = None
        for scores, v_ref, keys in pieces:
            lifted = jnp.exp(scores - highest)
            count = jnp.sum(lifted, axis=0, keepdims=True)
            summed = count if summed is None else summed + count
            part = dot(jnp.concatenate([v_ref[feats, keys], ones], axis=0), lifted.astype(BF), 1, 0)
            total = part if total is None else total + part
        context = total[:HD] / total[HD : HD + 1]
        ctx_ref[feats, :] = context.astype(BF)
        wide_ref[feats, :] = context
        lse_ref[0, head : head + 1, :] = highest + jnp.log(summed)


def attend_forward(q, k_own, k_par, v_own, v_par, bias):
    feats, rows = q.shape
    half = k_own.shape[1]
    groups = feats // GROUP
    block = 256
    side = pl.BlockSpec((GROUP, half), lambda b, g: (g, 0))
    lane = pl.BlockSpec((GROUP, block), lambda b, g: (g, b))
    return pl.pallas_call(
        attend_forward_kernel,
        grid=(rows // block, groups),
        in_specs=[lane, side, side, side, side, pl.BlockSpec((2 * half, block), lambda b, g: (0, b))],
        out_specs=[lane, lane, pl.BlockSpec((1, GROUP // HD, block), lambda b, g: (g, 0, b))],
        out_shape=[
            jax.ShapeDtypeStruct((feats, rows), BF),
            jax.ShapeDtypeStruct((feats, rows), F32),
            jax.ShapeDtypeStruct((groups, GROUP // HD, rows), F32),
        ],
        compiler_params=pltpu.CompilerParams(vmem_limit_bytes=40 * 1024 * 1024),
        cost_estimate=pl.CostEstimate(
            flops=16 * feats * rows * half, bytes_accessed=8 * feats * half, transcendentals=0
        ),
    )(q, k_own, k_par, v_own, v_par, bias)


def attend_backward_kernel(
    q_ref, ko_ref, kp_ref, vo_ref, vp_ref, bias_ref, ctx_ref, lse_ref, do_ref,
    dq_ref, dk_ref, dv_ref, dk_sum, dv_sum,
):
    half = ko_ref.shape[1]
    block = pl.program_id(1)

    @pl.when(block == 0)
    def _():
        dk_sum[...] = jnp.zeros_like(dk_sum)
        dv_sum[...] = jnp.zeros_like(dv_sum)

    for pair in range(q_ref.shape[0] // (2 * HD)):
        wide = pl.ds(pair * 2 * HD, 2 * HD)
        q_rows = q_ref[wide, :].T
        do_rows = do_ref[wide, :].T
        lanes = lax.broadcasted_iota(jnp.int32, q_rows.shape, 1) // HD
        for inner in range(2):
            head = 2 * pair + inner
            feats = pl.ds(head * HD, HD)
            query = q_ref[feats, :]
            grad = do_ref[feats, :]
            q_side = jnp.where(lanes == inner, q_rows, jnp.zeros_like(q_rows))
            do_side = jnp.where(lanes == inner, do_rows, jnp.zeros_like(do_rows))
            lse = lse_ref[0, head : head + 1, :]
            delta = jnp.sum(grad.astype(F32) * ctx_ref[feats, :], axis=0, keepdims=True)
            total = None
            for k_ref, v_ref, base in ((ko_ref, vo_ref, 0), (kp_ref, vp_ref, half)):
                keys = pl.ds(base, half)
                scores = dot(k_ref[feats, :], query, 0, 0) + bias_ref[keys, :]
                probs = jnp.exp(scores - lse)
                grad_probs = dot(v_ref[feats, :], grad, 0, 0)
                grad_scores = (probs * (grad_probs - delta)).astype(BF)
                dv_sum[keys, wide] += dot(probs.astype(BF), do_side, 1, 0)
                dk_sum[keys, wide] += dot(grad_scores, q_side, 1, 0)
                part = dot(k_ref[feats, :], grad_scores, 1, 0)
                total = part if total is None else total + part
            dq_ref[feats, :] = (total * (HD**-0.5)).astype(BF)

    @pl.when(block == pl.num_programs(1) - 1)
    def _():
        dk_ref[...] = dk_sum[...].astype(BF)
        dv_ref[...] = dv_sum[...].astype(BF)


def attend_backward(q, k_own, k_par, v_own, v_par, bias, ctx, lse, grad):
    feats, rows = q.shape
    half = k_own.shape[1]
    groups = feats // GROUP
    block = 256
    side = pl.BlockSpec((GROUP, half), lambda g, b: (g, 0))
    lane = pl.BlockSpec((GROUP, block), lambda g, b: (g, b))
    key_side = pl.BlockSpec((2 * half, GROUP), lambda g, b: (0, g))
    return pl.pallas_call(
        attend_backward_kernel,
        grid=(groups, rows // block),
        in_specs=[
            lane, side, side, side, side,
            pl.BlockSpec((2 * half, block), lambda g, b: (0, b)),
            lane,
            pl.BlockSpec((1, GROUP // HD, block), lambda g, b: (g, 0, b)),
            lane,
        ],
        out_specs=[lane, key_side, key_side],
        out_shape=[
            jax.ShapeDtypeStruct((feats, rows), BF),
            jax.ShapeDtypeStruct((2 * half, feats), BF),
            jax.ShapeDtypeStruct((2 * half, feats), BF),
        ],
        scratch_shapes=[pltpu.VMEM((2 * half, GROUP), F32)] * 2,
        compiler_params=pltpu.CompilerParams(vmem_limit_bytes=48 * 1024 * 1024),
        cost_estimate=pl.CostEstimate(
            flops=40 * feats * rows * half, bytes_accessed=16 * feats * half, transcendentals=0
        ),
    )(q, k_own, k_par, v_own, v_par, bias, ctx, lse, grad)


def layer_norm(z, norm):
    center = z - jnp.mean(z, axis=-1, keepdims=True)
    inverse = lax.rsqrt(jnp.mean(center * center, axis=-1, keepdims=True) + EPS)
    scaled = center * inverse
    return (scaled * norm[0] + norm[1], (scaled, inverse))


def norm_back(grad, kept, norm):
    scaled, inverse = kept
    inner = grad * norm[0]
    back = inverse * (
        inner
        - jnp.mean(inner, axis=-1, keepdims=True)
        - scaled * jnp.mean(inner * scaled, axis=-1, keepdims=True)
    )
    return (back, jnp.stack([jnp.sum(grad * scaled, axis=0), jnp.sum(grad, axis=0)]))


def gelu_both(raised):
    rise = 0.5 * (1.0 + lax.erf(raised * (0.5**0.5)))
    slope = rise + raised * jnp.exp(-0.5 * raised * raised) * 0.3989422804014327
    return ((raised * rise).astype(BF), slope.astype(BF))


def feature_major(weight, rows):
    out = jnp.einsum("tde,rd->ter", weight, rows, preferred_element_type=F32)
    return out.reshape(-1, rows.shape[0])


def heads_major(weight, rows):
    tall = rows.reshape(rows.shape[0], weight.shape[0], weight.shape[2])
    return jnp.einsum("rte,tde->rd", tall, weight, preferred_element_type=F32)


def from_features(weight, feats):
    tall = feats.reshape(weight.shape[0], weight.shape[2], feats.shape[1])
    return jnp.einsum("ter,tde->rd", tall, weight, preferred_element_type=F32)


def local(source, target, src_len, tgt_len, global_mask, attn_w, proj_w, cross_w, up_w, down_w, norms, dec_cot):
    section = lax.axis_index("section")
    y = lax.axis_index("ty")
    c = lax.axis_index("tc")
    src_rows = source.shape[1]
    tgt_rows = target.shape[1]
    width = source.shape[2]
    src_own = src_rows // 4
    tgt_own = tgt_rows // 4
    cut = attn_w.shape[1]
    head_cut = attn_w.shape[3]
    unit_cut = up_w.shape[2]

    def pick(array):
        return lax.dynamic_index_in_dim(array, section, 0, keepdims=False)

    def quarter(array, at_y, at_c):
        size = array.shape[0] // 4
        return lax.dynamic_slice_in_dim(array, (2 * at_y + at_c) * size, size, 0)

    def ordered(array):
        return jnp.concatenate(
            [quarter(array, y, c), quarter(array, 1 - y, c), quarter(array, y, 1 - c), quarter(array, 1 - y, 1 - c)]
        )

    src_length = pick(src_len)
    tgt_length = pick(tgt_len)
    src_place = ordered(jnp.arange(src_rows, dtype=jnp.int32))
    tgt_place = ordered(jnp.arange(tgt_rows, dtype=jnp.int32))
    marks = ordered(pick(global_mask)) > 0
    src_mine = src_place[:src_own]
    tgt_mine = tgt_place[:tgt_own]
    src_valid = (src_mine < src_length).astype(F32)[:, None]
    tgt_valid = (tgt_mine < tgt_length).astype(F32)[:, None]

    def bias_of(allowed):
        return jnp.where(allowed, 0.0, MASKED).astype(F32)

    near = jnp.abs(src_place[:, None] - src_mine[None, :]) <= WINDOW // 2
    enc_bias = bias_of((near | marks[:, None] | marks[None, :src_own]) & (src_place < src_length)[:, None])
    dec_bias = bias_of((tgt_place[:, None] <= tgt_mine[None, :]) & (tgt_place < tgt_length)[:, None])
    cross_bias = bias_of(jnp.broadcast_to((src_place < src_length)[:, None], (src_rows, tgt_own)))

    def gather(shard):
        full = lax.all_gather(shard, EVERY, tiled=True)
        return full.reshape(2, 4, width, shard.shape[1])

    attn_all = gather(jnp.concatenate([attn_w.reshape(cut, 3 * head_cut), proj_w[0].T], axis=1))
    feed_all = gather(jnp.concatenate([up_w.reshape(cut, unit_cut), down_w[0].T], axis=1))
    cross_all = gather(cross_w.reshape(cut, 2 * head_cut))
    norms_all = lax.all_gather(norms, "section", tiled=True)

    def layer(index):
        attn = attn_all[index]
        q = attn[:, :, :head_cut]
        k = attn[:, :, head_cut : 2 * head_cut]
        v = attn[:, :, 2 * head_cut : 3 * head_cut]
        proj = attn[:, :, 3 * head_cut :]
        up = feed_all[index][:, :, :unit_cut]
        down = feed_all[index][:, :, unit_cut:]
        first = cross_all[index][:, :, :head_cut]
        second = cross_all[index][:, :, head_cut:]
        return (q, k, v, proj, up, down, first, second)

    q_e, k_e, v_e, proj_e, up_e, down_e, ck_e, cv_e = layer(0)
    q_d, k_d, v_d, proj_d, up_d, down_d, cq_d, co_d = layer(1)
    norm_e = norms_all[0]
    norm_d = norms_all[1]
    scale = HD**-0.5

    def queries(weight, rows):
        return feature_major(weight, rows).astype(BF) * jnp.asarray(scale, BF)

    def key_values(k_weight, v_weight, rows):
        own = jnp.concatenate([feature_major(k_weight, rows), feature_major(v_weight, rows)]).astype(BF)
        par = swap(own, "tc")
        return (own[:width], par[:width], own[width:], par[width:])

    def feed_forward(low, up, down):
        raised = jnp.einsum("rd,tdu->rtu", low, up, preferred_element_type=F32)
        active, slope = gelu_both(raised)
        return (active, slope, jnp.einsum("rtu,tdu->rd", active, down, preferred_element_type=F32))

    def feed_back(low, active, slope, lowered_grad, up, down):
        grad_active = jnp.einsum("rd,tdu->rtu", lowered_grad, down, preferred_element_type=F32)
        raised_grad = (grad_active * slope.astype(F32)).astype(BF)
        grad_down = jnp.einsum("rd,rtu->tdu", lowered_grad, active, preferred_element_type=F32)
        grad_up = jnp.einsum("rd,rtu->tdu", low, raised_grad, preferred_element_type=F32)
        back = jnp.einsum("rtu,tdu->rd", raised_grad, up, preferred_element_type=F32)
        return (back, grad_up, grad_down)

    def split(rows):
        return rows.reshape(rows.shape[0], 4, rows.shape[1] // 4)

    def split_feats(feats):
        return feats.reshape(4, feats.shape[0] // 4, feats.shape[1])

    def chip_sum(dk, dv):
        half = dk.shape[0] // 2
        other = swap(jnp.concatenate([dk[half:], dv[half:]], axis=1), "tc")
        own = jnp.concatenate([dk[:half], dv[:half]], axis=1)
        total = (own.astype(F32) + other.astype(F32)).astype(BF)
        return (total[:, :width], total[:, width:])

    def chip_rows(k_weight, v_weight, dk, dv):
        partial_rows = heads_major(k_weight, dk) + heads_major(v_weight, dv)
        mine = partial_rows.shape[0] // 2
        return (partial_rows[:mine], swap(partial_rows[mine:].astype(BF), "ty").astype(F32))

    src = pick(source)
    src_set = jnp.concatenate([quarter(src, y, c), quarter(src, 1 - y, c)]).astype(F32)
    normed, kept = layer_norm(src_set, norm_e[0])
    enc_kept_zero = (kept[0][:src_own], kept[1][:src_own])
    normed_low = normed.astype(BF)
    normed_mine = normed[:src_own]
    low_mine = normed_low[:src_own]
    enc_q = queries(q_e, low_mine)
    enc_kv = key_values(k_e, v_e, normed_low)
    enc_ctx, enc_wide, enc_lse = attend_forward(enc_q, *enc_kv, enc_bias)
    middle, enc_kept_one = layer_norm(normed_mine + from_features(proj_e, enc_ctx), norm_e[1])
    middle_low = middle.astype(BF)
    enc_active, enc_slope, lowered = feed_forward(middle_low, up_e, down_e)
    memory, enc_kept_two = layer_norm(middle + lowered, norm_e[2])
    memory_low = (memory * src_valid).astype(BF)
    memory_set = jnp.concatenate([memory_low, swap(memory_low, "ty")])
    mem_kv = key_values(ck_e, cv_e, memory_set)

    tgt = pick(target)
    tgt_set = jnp.concatenate([quarter(tgt, y, c), quarter(tgt, 1 - y, c)])
    tgt_low = tgt_set[:tgt_own]
    dec_q = queries(q_d, tgt_low)
    dec_kv = key_values(k_d, v_d, tgt_set)
    dec_ctx, dec_wide, dec_lse = attend_forward(dec_q, *dec_kv, dec_bias)
    first, dec_kept_zero = layer_norm(tgt_low.astype(F32) + from_features(proj_d, dec_ctx), norm_d[0])
    first_low = first.astype(BF)
    asking = queries(cq_d, first_low)
    crossed, cross_wide, cross_lse = attend_forward(asking, *mem_kv, cross_bias)
    second, dec_kept_one = layer_norm(first + from_features(co_d, crossed), norm_d[1])
    second_low = second.astype(BF)
    dec_active, dec_slope, lowered = feed_forward(second_low, up_d, down_d)
    result, dec_kept_two = layer_norm(second + lowered, norm_d[2])
    output = (result * tgt_valid).astype(BF)

    cotangent = quarter(pick(dec_cot), y, c).astype(F32) * tgt_valid
    back_two, dnorm_d2 = norm_back(cotangent, dec_kept_two, norm_d[2])
    lowered_grad = back_two.astype(BF)
    back, grad_up_d, grad_down_d = feed_back(second_low, dec_active, dec_slope, lowered_grad, up_d, down_d)
    back_one, dnorm_d1 = norm_back(back_two + back, dec_kept_one, norm_d[1])
    answer_grad = back_one.astype(BF)
    grad_co = jnp.einsum("rd,ter->tde", answer_grad, split_feats(crossed), preferred_element_type=F32)
    crossed_grad = feature_major(co_d, answer_grad).astype(BF)
    asking_grad, mem_dk, mem_dv = attend_backward(asking, *mem_kv, cross_bias, cross_wide, cross_lse, crossed_grad)
    mem_dk, mem_dv = chip_sum(mem_dk, mem_dv)
    grad_cq = jnp.einsum("rd,ter->tde", first_low, split_feats(asking_grad), preferred_element_type=F32)
    back_zero, dnorm_d0 = norm_back(back_one + from_features(cq_d, asking_grad), dec_kept_zero, norm_d[0])
    mixed_grad = back_zero.astype(BF)
    grad_proj_d = jnp.einsum("rd,ter->tde", mixed_grad, split_feats(dec_ctx), preferred_element_type=F32)
    ctx_grad = feature_major(proj_d, mixed_grad).astype(BF)
    dq, dk, dv = attend_backward(dec_q, *dec_kv, dec_bias, dec_wide, dec_lse, ctx_grad)
    dk, dv = chip_sum(dk, dv)
    grad_attn_d = jnp.concatenate(
        [
            jnp.einsum("rd,ter->tde", tgt_low, split_feats(dq), preferred_element_type=F32),
            jnp.einsum("rd,rte->tde", tgt_set, split(dk), preferred_element_type=F32),
            jnp.einsum("rd,rte->tde", tgt_set, split(dv), preferred_element_type=F32),
        ],
        axis=2,
    )
    mine, other = chip_rows(k_d, v_d, dk, dv)
    target_grad = (back_zero + mine + other + from_features(q_d, dq)).astype(BF)

    grad_cross_e = jnp.concatenate(
        [
            jnp.einsum("rd,rte->tde", memory_set, split(mem_dk), preferred_element_type=F32),
            jnp.einsum("rd,rte->tde", memory_set, split(mem_dv), preferred_element_type=F32),
        ],
        axis=2,
    )
    mine, other = chip_rows(ck_e, cv_e, mem_dk, mem_dv)
    back_two, dnorm_e2 = norm_back((mine + other) * src_valid, enc_kept_two, norm_e[2])
    lowered_grad = back_two.astype(BF)
    back, grad_up_e, grad_down_e = feed_back(middle_low, enc_active, enc_slope, lowered_grad, up_e, down_e)
    back_one, dnorm_e1 = norm_back(back_two + back, enc_kept_one, norm_e[1])
    mixed_grad = back_one.astype(BF)
    grad_proj_e = jnp.einsum("rd,ter->tde", mixed_grad, split_feats(enc_ctx), preferred_element_type=F32)
    ctx_grad = feature_major(proj_e, mixed_grad).astype(BF)
    dq, dk, dv = attend_backward(enc_q, *enc_kv, enc_bias, enc_wide, enc_lse, ctx_grad)
    dk, dv = chip_sum(dk, dv)
    grad_attn_e = jnp.concatenate(
        [
            jnp.einsum("rd,ter->tde", low_mine, split_feats(dq), preferred_element_type=F32),
            jnp.einsum("rd,rte->tde", normed_low, split(dk), preferred_element_type=F32),
            jnp.einsum("rd,rte->tde", normed_low, split(dv), preferred_element_type=F32),
        ],
        axis=2,
    )
    mine, other = chip_rows(k_e, v_e, dk, dv)
    back_zero, dnorm_e0 = norm_back(back_one + mine + other + from_features(q_e, dq), enc_kept_zero, norm_e[0])
    source_grad = back_zero.astype(BF)

    def scatter(enc, dec):
        both = jnp.stack([enc, dec]).astype(BF).reshape(-1, enc.shape[2])
        return lax.psum_scatter(both, EVERY, tiled=True).astype(F32)

    attn_sum = scatter(
        jnp.concatenate([grad_attn_e, grad_proj_e], axis=2), jnp.concatenate([grad_attn_d, grad_proj_d], axis=2)
    )
    feed_sum = scatter(
        jnp.concatenate([grad_up_e, grad_down_e], axis=2), jnp.concatenate([grad_up_d, grad_down_d], axis=2)
    )
    cross_sum = scatter(grad_cross_e, jnp.concatenate([grad_cq, grad_co], axis=2))
    norm_sum = lax.psum(
        jnp.stack([jnp.stack([dnorm_e0, dnorm_e1, dnorm_e2]), jnp.stack([dnorm_d0, dnorm_d1, dnorm_d2])]), EVERY
    )
    norm_share = lax.dynamic_slice(
        norm_sum, (section, 0, 0, lax.axis_index("dp") * cut), (1, 3, 2, cut)
    )

    def everyone(rows):
        full = lax.all_gather(rows, ("section", "ty", "tc"), tiled=True)
        return full.reshape(2, -1, width)

    return (
        everyone(output),
        everyone(source_grad),
        everyone(target_grad),
        attn_sum[:, : 3 * head_cut].reshape(1, cut, 3, head_cut),
        attn_sum[:, 3 * head_cut :].T[None],
        cross_sum.reshape(1, cut, 2, head_cut),
        feed_sum[None, :, :unit_cut],
        feed_sum[:, unit_cut:].T[None],
        norm_share,
    )


def solution(mesh):
    shape = mesh.devices.shape
    fine = Mesh(mesh.devices.reshape(shape[0], shape[1], 2, 2), ("section", "dp", "ty", "tc"))
    tensor = ("ty", "tc")
    return jax.shard_map(
        local,
        mesh=fine,
        in_specs=(
            P("dp", None, None),
            P("dp", None, None),
            P("dp"),
            P("dp"),
            P("dp", None),
            P("section", "dp", None, tensor),
            P("section", tensor, "dp"),
            P("section", "dp", None, tensor),
            P("section", "dp", tensor),
            P("section", tensor, "dp"),
            P("section", None, None, None),
            P("dp", None, None),
        ),
        out_specs=(
            P("dp", None, None),
            P("dp", None, None),
            P("dp", None, None),
            P("section", "dp", None, tensor),
            P("section", tensor, "dp"),
            P("section", "dp", None, tensor),
            P("section", "dp", tensor),
            P("section", tensor, "dp"),
            P("section", None, None, "dp"),
        ),
        check_vma=False,
    )
```

time: 3300 us -> 1120 us (0.34)
  waiting for transfers between devices: 1600 us -> 576 us
  matrix products: 766 us -> 115 us
  other arithmetic: 492 us -> 76.4 us
  Pallas kernels: 0 us -> 113 us
  local copies, waits for them, and re-layouts: 257 us -> 164 us
  loops' own time: 56 us -> 0 us
  blocking collectives: 90.8 us -> 44.9 us
    psum x9 -> x0, waiting for transfers between devices: 1290 us -> none  [the longest x5 593 us: head_total(): lax.psum(partial_value.astype(jnp.bfloat16), 'tensor').astype(jnp.float32)]
    dot_general x92 -> x44, matrix products: 654 us -> 111 us  [the longest x6 20.3 us: heads_major(): return jnp.einsum('rte,tde->rd', tall, weight, preferred_element_type=F32)]
    reduce_scatter x2 -> x3, waiting for transfers between devices: 0.01 us -> 334 us  [scatter(): return lax.psum_scatter(both, EVERY, tiled=True).astype(F32)]
    ppermute x2 -> x10, waiting for transfers between devices: 313 us -> 50.8 us  [swap(): return lax.ppermute(value, axis, [(0, 1), (1, 0)])]
    all_gather x2 -> x6, waiting for transfers between devices: 0.04 us -> 191 us  [the longest x3 191 us: gather(): full = lax.all_gather(shard, EVERY, tiled=True)]
    convert_element_type x55 -> x11, other arithmetic: 188 us -> 17.4 us  [the longest x3 8.38 us: chip_sum(): total = (own.astype(F32) + other.astype(F32)).astype(BF)]
    pallas_call x0 -> x6, Pallas kernels: none -> 113 us  [the longest x3 66.8 us: attend_backward(): pl.pallas_call(attend_backward_kernel, grid=(groups, rows // block), in_s...]
    all_gather x3 -> x1, blocking collectives: 90.8 us -> 5.33 us  [local(): norms_all = lax.all_gather(norms, 'section', tiled=True)]
  transfers between devices with their start and end apart: 19 -> 19, of which waited for: 10 -> 9; matrix products, arithmetic and copies ran while one was open for 19% -> 25% of each run, Pallas kernels for 0% -> 7%
where the time goes in v1:
time: 1120 us; the launch traced here: 1110 us
  waiting for transfers between devices  576 us (51%)
  local copies, waits for them, and re-layouts  164 us (15%)
  matrix products  115 us (10%)
  Pallas kernels  113 us (10%)
  other arithmetic  76.4 us (7%)
  blocking collectives  44.9 us (4%)
  between operations  17 us (2%)
    reduce_scatter x3, waiting for transfers between devices, scatter(): return lax.psum_scatter(both, EVERY, tiled=True).astype(F32)  334 us
    all_gather x3, waiting for transfers between devices, gather(): full = lax.all_gather(shard, EVERY, tiled=True)  191 us
    pallas_call x3, Pallas kernels, attend_backward(): pl.pallas_call(attend_backward_kernel, grid=(groups, rows // block), in_s...  66.8 us
    ppermute x10, waiting for transfers between devices, swap(): return lax.ppermute(value, axis, [(0, 1), (1, 0)])  50.8 us
    unnamed x354, local copies, waits for them, and re-layouts  48.6 us
    pallas_call x3, Pallas kernels, attend_forward(): pl.pallas_call(attend_forward_kernel, grid=(rows // block, groups), in_sp...  45.9 us
    another operation x3, local copies, waits for them, and re-layouts, scatter(): both = jnp.stack([enc, dec]).astype(BF).reshape(-1, enc.shape[2])  44.1 us
    psum x1, blocking collectives, local(): lax.psum(jnp.stack([jnp.stack([dnorm_e0, dnorm_e1, dnorm_e2]), jnp.stack(...  39.6 us
  transfers between devices with their start and end apart: 19, of which 9 were waited for; matrix products, arithmetic and copies ran while one was open for 25% of the time, Pallas kernels for 7%

profile of v1, /device:TPU:0, one launch (start us, length us, event | category | flops | bytes accessed | tf_op | source)
XLA Modules:
  0.0 1112.6 jit_solution(9055052328423734971)
XLA Ops:
  24.5 71.8 %all-gather.7.cloned.1.call-done = bf16[6144,768]{1,0:T(8,128)(2,1)} async-done(((bf16[192,768]{1,0:T(8,128)(2,1)}), bf16[6144,768]{1,0:T(8,128)(2,1)}) %all-gather.7.cloned.1.call-update) | async-done | bytes 9437200 | tf_op jit(solution)/shard_map/all_gather | solution.py:240
  96.3 6.5 fusion.195
  122.0 40.0 %all-gather.9.cloned.1.call-done = bf16[6144,384]{1,0:T(8,128)(2,1)} async-done(((bf16[192,384]{1,0:T(8,128)(2,1)}), bf16[6144,384]{1,0:T(8,128)(2,1)}) %all-gather.9.cloned.1.call-update) | async-done | bytes 4718608 | tf_op jit(solution)/shard_map/all_gather | solution.py:240
  180.0 25.7 %shard_map.188 = (bf16[768,512]{1,0:T(8,128)(2,1)S(1)}, f32[768,512]{1,0:T(8,128)S(1)}, f32[3,4,512]{2,1,0:T(4,128)S(1)}) custom-call(bf16[768,512]{1,0:T(8,128)(2,1)S(1)} %bitcast.365, bf16[768,1024]{1,0:T(8,128)(2,1)S(1)} %bitcast.342, bf16[768,1024]{1,0:T(8,128)(2,1)S(1)} %get-tuple-element.127.kp_ref, bf16[768,1024]{1,0:T(8,128)(2,1)S(1)} %bitcast.345, ...), custom_call_target="tpu_custom_call" | custom-call | flops 6442450944 | bytes 6291456 | tf_op jit(solution)/shard_map/pallas_call | solution.py:63
  210.1 78.9 %all-gather.11.cloned.1.call-done = bf16[6144,1536]{1,0:T(8,128)(2,1)} async-done(((bf16[192,1536]{1,0:T(8,128)(2,1)}), bf16[6144,1536]{1,0:T(8,128)(2,1)}) %all-gather.11.cloned.1.call-update) | async-done | bytes 18874384 | tf_op jit(solution)/shard_map/all_gather | solution.py:240
  289.0 11.4 %fusion.194 = (bf16[3072,1536]{1,0:T(8,128)(2,1)S(1)}, bf16[3072,1536]{1,0:T(8,128)(2,1)}) fusion(bf16[6144,1536]{1,0:T(8,128)(2,1)} %all-gather.11.cloned.1.call-done), kind=kLoop, calls=%fused_computation.316 | loop fusion | bytes 37748736 | tf_op jit(solution)/shard_map/slice | solution.py:254
  300.4 5.9 multiply_convert_fusion.1
  315.5 14.2 %collective-permute-done.2 = bf16[512,768]{1,0:T(8,128)(2,1)S(1)} collective-permute-done((bf16[512,768]{1,0:T(8,128)(2,1)S(1)}, bf16[512,768]{1,0:T(8,128)(2,1)S(1)}, u32[]{:S(2)}, u32[]{:S(2)}) %collective-permute-start.2) | collective-permute-done | bytes 786464 | tf_op jit(solution)/shard_map/ppermute | solution.py:23
  361.3 7.2 shard_map.187
  374.9 13.0 %shard_map.189 = (bf16[768,256]{1,0:T(8,128)(2,1)S(1)}, f32[768,256]{1,0:T(8,128)S(1)}, f32[3,4,256]{2,1,0:T(4,128)S(1)}) custom-call(bf16[768,256]{1,0:T(8,128)(2,1)S(1)} %bitcast.360, bf16[768,1024]{1,0:T(8,128)(2,1)S(1)} %bitcast.337, bf16[768,1024]{1,0:T(8,128)(2,1)S(1)} %get-tuple-element.125.kp_ref, bf16[768,1024]{1,0:T(8,128)(2,1)S(1)} %bitcast.334, ...), custom_call_target="tpu_custom_call" | custom-call | flops 3221225472 | bytes 6291456 | tf_op jit(solution)/shard_map/pallas_call | solution.py:63
  408.0 19.6 %shard_map.190 = (bf16[768,256]{1,0:T(8,128)(2,1)S(1)}, bf16[2048,768]{1,0:T(8,128)(2,1)}, bf16[2048,768]{1,0:T(8,128)(2,1)}) custom-call(bf16[768,256]{1,0:T(8,128)(2,1)S(1)} %bitcast.361, bf16[768,1024]{1,0:T(8,128)(2,1)S(1)} %bitcast.338, bf16[768,1024]{1,0:T(8,128)(2,1)S(1)} %get-tuple-element.125.kp_ref, bf16[768,1024]{1,0:T(8,128)(2,1)} %bitcast.335, ...), custom_call_target="tpu_custom_call" | custom-call | flops 8053063680 | bytes 12582912 | tf_op jit(solution)/shard_map/pallas_call | solution.py:133
  439.7 9.5 shard_map.192
  491.4 17.3 %collective-permute-done.5 = bf16[512,768]{1,0:T(8,128)(2,1)} collective-permute-done((bf16[512,768]{1,0:T(8,128)(2,1)S(1)}, bf16[512,768]{1,0:T(8,128)(2,1)}, u32[]{:S(2)}, u32[]{:S(2)}) %collective-permute-start.5) | collective-permute-done | bytes 786464 | tf_op jit(solution)/shard_map/ppermute | solution.py:23
  512.4 8.0 multiply_convert_fusion
  527.7 37.7 %shard_map.191 = (bf16[768,512]{1,0:T(8,128)(2,1)S(1)}, bf16[2048,768]{1,0:T(8,128)(2,1)}, bf16[2048,768]{1,0:T(8,128)(2,1)}) custom-call(bf16[768,512]{1,0:T(8,128)(2,1)S(1)} %bitcast.366, bf16[768,1024]{1,0:T(8,128)(2,1)S(1)} %bitcast.343, bf16[768,1024]{1,0:T(8,128)(2,1)S(1)} %copy-done.8, bf16[768,1024]{1,0:T(8,128)(2,1)} %bitcast.346, ...), custom_call_target="tpu_custom_call" | custom-call | flops 16106127360 | bytes 12582912 | tf_op jit(solution)/shard_map/pallas_call | solution.py:133
  580.2 6.7 copy.91
  607.4 17.6 %collective-permute-done.7 = bf16[512,768]{1,0:T(8,128)(2,1)S(1)} collective-permute-done((bf16[512,768]{1,0:T(8,128)(2,1)S(1)}, bf16[512,768]{1,0:T(8,128)(2,1)S(1)}, u32[]{:S(2)}, u32[]{:S(2)}) %collective-permute-start.7) | collective-permute-done | bytes 786464 | tf_op jit(solution)/shard_map/ppermute | solution.py:23
  644.5 8.5 pad_maximum_fusion.1
  653.0 12.7 %copy.89 = bf16[2,4,768,768]{3,2,1,0:T(8,128)(2,1)} copy(bf16[2,4,768,768]{2,3,1,0:T(8,128)(2,1)} %pad_maximum_fusion.1) | data formatting | bytes 18874368 | tf_op jit(solution)/shard_map/stack | solution.py:397
  681.1 8.1 pad_maximum_fusion
  689.3 24.7 %copy.96 = bf16[2,4,768,1536]{3,2,1,0:T(8,128)(2,1)} copy(bf16[2,4,768,1536]{2,3,1,0:T(8,128)(2,1)} %pad_maximum_fusion) | data formatting | bytes 37748736 | tf_op jit(solution)/shard_map/stack | solution.py:397
  715.1 39.6 %psum.7 = f32[2,3,2,768]{3,2,1,0:T(2,128)S(1)} all-reduce(f32[2,3,2,768]{3,2,1,0:T(2,128)S(1)} %pad_maximum_fusion.13), channel_id=1, replica_groups=mesh['section'=2,'dp'=4,'ty'=2,'tc'=2] {'section','ty','tc','dp'}, use_global_device_ids=true, to_apply=%region_39.40 | all-reduce | flops 9216 | bytes 73728 | tf_op jit(solution)/shard_map/psum | solution.py:407
  757.4 125.2 %reduce-scatter.4.cloned.1.call-done = bf16[192,768]{1,0:T(8,128)(2,1)} async-done(((bf16[6144,768]{1,0:T(8,128)(2,1)}), bf16[192,768]{1,0:T(8,128)(2,1)}) %reduce-scatter.4.cloned.1.call-update) | async-done | bytes 294928 | tf_op jit(solution)/shard_map/reduce_scatter | solution.py:398
  885.9 208.8 %reduce-scatter.8.cloned.1.call-done = bf16[192,1536]{1,0:T(8,128)(2,1)} async-done(((bf16[6144,1536]{1,0:T(8,128)(2,1)}), bf16[192,1536]{1,0:T(8,128)(2,1)}) %reduce-scatter.8.cloned.1.call-update) | async-done | bytes 589840 | tf_op jit(solution)/shard_map/reduce_scatter | solution.py:398
  (588 shorter events, 276.9 us)
Async XLA Ops:
  7.2 89.1 %all-gather.7.cloned.1.call-start = ((), (), s32[]{:S(2)}) async-start(), calls=%async_computation.3 | async-start | bytes 9732096 | tf_op jit(solution)/shard_map/all_gather | solution.py:240
  10.3 151.7 %all-gather.9.cloned.1.call-start = ((), (), s32[]{:S(2)}) async-start(), calls=%async_computation.4 | async-start | bytes 4866048 | tf_op jit(solution)/shard_map/all_gather | solution.py:240
  11.2 277.8 %all-gather.11.cloned.1.call-start = ((), (), s32[]{:S(2)}) async-start(), calls=%async_computation.5 | async-start | bytes 19464192 | tf_op jit(solution)/shard_map/all_gather | solution.py:240
  12.2 702.8 %all-gather.13.cloned.1.call-start = ((), (), s32[]{:S(2)}) async-start(), calls=%async_computation.6 | async-start | bytes 3538944 | tf_op jit(solution)/shard_map/all_gather | solution.py:415
  20.3 381.1 %copy-start.95 = (f32[768]{0:T(1024)}, f32[768]{0:T(1024)S(1)}, u32[]{:S(2)}) copy-start(f32[768]{0:T(1024)S(1)} %get-tuple-element.87) | copy-start | bytes 9220
  111.3 65.2 %collective-permute-start.1 = (bf16[1536,1024]{1,0:T(8,128)(2,1)}, bf16[1536,1024]{1,0:T(8,128)(2,1)}, u32[]{:S(2)}, u32[]{:S(2)}) collective-permute-start(bf16[1536,1024]{1,0:T(8,128)(2,1)} %pad_maximum_fusion.3), channel_id=1, source_target_pairs={{0,1},{1,0},{2,3},{3,2},{4,5},{5,4},{6,7},{7,6},{8,9},{9,8},{10,11... | collective-permute-start | bytes 9437192 | tf_op jit(solution)/shard_map/ppermute | solution.py:23
  117.5 195.2 %copy-start.87 = (bf16[256,768]{1,0:T(8,128)(2,1)}, bf16[256,768]{1,0:T(8,128)(2,1)S(1)}, u32[]{:S(2)}) copy-start(bf16[256,768]{1,0:T(8,128)(2,1)S(1)} %get-tuple-element.128) | copy-start | bytes 1179652
  209.7 96.6 %copy-start.49 = (f32[512,768]{1,0:T(8,128)}, f32[512,768]{1,0:T(8,128)S(1)}, u32[]{:S(2)}) copy-start(f32[512,768]{1,0:T(8,128)S(1)} %get-tuple-element.155) | copy-start | bytes 4718596
  209.7 96.6 %copy-start.109 = (f32[512]{0:T(512)}, f32[512]{0:T(512)S(1)}, u32[]{:S(2)}) copy-start(f32[512]{0:T(512)S(1)} %broadcast_multiply_fusion.8) | copy-start | bytes 6148
  309.9 19.8 %collective-permute-start.2 = (bf16[512,768]{1,0:T(8,128)(2,1)S(1)}, bf16[512,768]{1,0:T(8,128)(2,1)S(1)}, u32[]{:S(2)}, u32[]{:S(2)}) collective-permute-start(bf16[512,768]{1,0:T(8,128)(2,1)S(1)} %multiply_convert_fusion.5), channel_id=1, source_target_pairs={{0,2},{2,0},{1,3},{3,1},{4,6},{6,4},{5,7},{7,5},{8,10},{10,8},{9,1... | collective-permute-start | bytes 2359304 | tf_op jit(solution)/shard_map/ppermute | solution.py:23
  315.5 44.1 %collective-permute-start = (bf16[1536,512]{1,0:T(8,128)(2,1)}, bf16[1536,512]{1,0:T(8,128)(2,1)}, u32[]{:S(2)}, u32[]{:S(2)}) collective-permute-start(bf16[1536,512]{1,0:T(8,128)(2,1)} %pad_maximum_fusion.7), channel_id=1, source_target_pairs={{0,1},{1,0},{2,3},{3,2},{4,5},{5,4},{6,7},{7,6},{8,9},{9,8},{10,11... | collective-permute-start | bytes 4718600 | tf_op jit(solution)/shard_map/ppermute | solution.py:23
  336.2 36.0 %collective-permute-start.3 = (bf16[1536,1024]{1,0:T(8,128)(2,1)}, bf16[1536,1024]{1,0:T(8,128)(2,1)}, u32[]{:S(2)}, u32[]{:S(2)}) collective-permute-start(bf16[1536,1024]{1,0:T(8,128)(2,1)} %pad_maximum_fusion.4), channel_id=1, source_target_pairs={{0,1},{1,0},{2,3},{3,2},{4,5},{5,4},{6,7},{7,6},{8,9},{9,8},{10,11... | collective-permute-start | bytes 9437192 | tf_op jit(solution)/shard_map/ppermute | solution.py:23
  434.3 34.3 %collective-permute-start.4 = (bf16[1024,1536]{1,0:T(8,128)(2,1)}, bf16[1024,1536]{1,0:T(8,128)(2,1)}, u32[]{:S(2)}, u32[]{:S(2)}) collective-permute-start(bf16[1024,1536]{1,0:T(8,128)(2,1)} %pad_maximum_fusion.5), channel_id=1, source_target_pairs={{0,1},{1,0},{2,3},{3,2},{4,5},{5,4},{6,7},{7,6},{8,9},{9,8},{10,11... | collective-permute-start | bytes 9437192 | tf_op jit(solution)/shard_map/ppermute | solution.py:23
  453.4 3.9 collective-permute-start.8
  454.0 261.1 %all-gather.17.cloned.1.call-start = ((), (), s32[]{:S(2)}) async-start(), calls=%async_computation.8 | async-start | bytes 3538944 | tf_op jit(solution)/shard_map/all_gather | solution.py:415
  467.1 20.5 %collective-permute-start.9 = (bf16[256,768]{1,0:T(8,128)(2,1)}, bf16[256,768]{1,0:T(8,128)(2,1)S(1)}, u32[]{:S(2)}, u32[]{:S(2)}) collective-permute-start(bf16[256,768]{1,0:T(8,128)(2,1)} %slice.550), channel_id=1, source_target_pairs={{0,2},{2,0},{1,3},{3,1},{4,6},{6,4},{5,7},{7,5},{8,10},{10,8},{9,1... | collective-permute-start | bytes 1179656 | tf_op jit(solution)/shard_map/ppermute | solution.py:23
  484.8 23.8 %collective-permute-start.5 = (bf16[512,768]{1,0:T(8,128)(2,1)S(1)}, bf16[512,768]{1,0:T(8,128)(2,1)}, u32[]{:S(2)}, u32[]{:S(2)}) collective-permute-start(bf16[512,768]{1,0:T(8,128)(2,1)S(1)} %slice.549), channel_id=1, source_target_pairs={{0,2},{2,0},{1,3},{3,1},{4,6},{6,4},{5,7},{7,5},{8,10},{10,8},{9,1... | collective-permute-start | bytes 2359304 | tf_op jit(solution)/shard_map/ppermute | solution.py:23
  491.3 264.0 %reduce-scatter.6.cloned.1.call-start = ((), (), s32[]{:S(2)}) async-start(), calls=%async_computation.10 | async-start | bytes 4866048 | tf_op jit(solution)/shard_map/reduce_scatter | solution.py:398
  572.1 14.9 %collective-permute-start.6 = (bf16[1024,1536]{1,0:T(8,128)(2,1)}, bf16[1024,1536]{1,0:T(8,128)(2,1)}, u32[]{:S(2)}, u32[]{:S(2)}) collective-permute-start(bf16[1024,1536]{1,0:T(8,128)(2,1)} %pad_maximum_fusion.6), channel_id=1, source_target_pairs={{0,1},{1,0},{2,3},{3,2},{4,5},{5,4},{6,7},{7,6},{8,9},{9,8},{10,11... | collective-permute-start | bytes 9437192 | tf_op jit(solution)/shard_map/ppermute | solution.py:23
  586.9 170.5 %all-gather.15.cloned.1.call-start = ((), (), s32[]{:S(2)}) async-start(), calls=%async_computation.7 | async-start | bytes 7077888 | tf_op jit(solution)/shard_map/all_gather | solution.py:415
  606.1 19.0 %collective-permute-start.7 = (bf16[512,768]{1,0:T(8,128)(2,1)S(1)}, bf16[512,768]{1,0:T(8,128)(2,1)S(1)}, u32[]{:S(2)}, u32[]{:S(2)}) collective-permute-start(bf16[512,768]{1,0:T(8,128)(2,1)S(1)} %slice.548), channel_id=1, source_target_pairs={{0,2},{2,0},{1,3},{3,1},{4,6},{6,4},{5,7},{7,5},{8,10},{10,8},{9,1... | collective-permute-start | bytes 2359304 | tf_op jit(solution)/shard_map/ppermute | solution.py:23
  630.0 252.6 %reduce-scatter.4.cloned.1.call-start = ((), (), s32[]{:S(2)}) async-start(), calls=%async_computation.9 | async-start | bytes 9732096 | tf_op jit(solution)/shard_map/reduce_scatter | solution.py:398
  665.9 428.8 %reduce-scatter.8.cloned.1.call-start = ((), (), s32[]{:S(2)}) async-start(), calls=%async_computation.11 | async-start | bytes 19464192 | tf_op jit(solution)/shard_map/reduce_scatter | solution.py:398
  883.9 214.9 %slice-start.8 = ((s8[6291456]{0:T(1024)(128)(4,1)}), s8[2097152]{0:T(1024)(128)(4,1)S(1)}, s32[]{:S(2)}) async-start(s8[6291456]{0:T(1024)(128)(4,1)} %bitcast.409), calls=%async_computation.20 | async-start | bytes 4194304
  (166 other events, 1576.7 us)
Sparse Core Ops, SparseCore 0:
  11.5 84.7 all-gather.6
  99.8 62.1 all-gather.8
  165.5 123.4 all-gather.10
  454.1 34.7 all-gather.12
  491.5 33.1 all-gather.16
  587.0 105.3 reduce-scatter.5
  695.1 45.2 all-gather.14
  747.3 135.2 reduce-scatter.3
  889.0 205.6 reduce-scatter.7

commit v2 on v1

v2 whole, which is shorter than its diff:
```python
import functools

import jax
import jax.numpy as jnp
from jax import lax
from jax.experimental import pallas as pl
from jax.experimental.pallas import tpu as pltpu
from jax.sharding import Mesh, PartitionSpec as P

HD = 64
WINDOW = 1024
EPS = 1e-05
MASKED = -1000000000.0
BF = jnp.bfloat16
F32 = jnp.float32
BLOCK = 256


def dot(a, b, ca, cb):
    return lax.dot_general(a, b, (((ca,), (cb,)), ((), ())), preferred_element_type=F32)


def fill_bias(mode, seg, place_ref, key_bias_ref, key_mark_ref, q_mark_ref, bias_ref):
    lanes = bias_ref.shape[1]
    for at in range(0, bias_ref.shape[0], seg):
        keys = pl.ds(at, seg)
        key_bias = key_bias_ref[keys, :]
        if mode == "all":
            bias_ref[keys, :] = jnp.broadcast_to(key_bias, (seg, lanes))
            continue
        key_place = place_ref[at // seg] + lax.broadcasted_iota(jnp.int32, (seg, lanes), 0)
        query_place = place_ref[4 + pl.program_id(0)] + lax.broadcasted_iota(jnp.int32, (seg, lanes), 1)
        if mode == "causal":
            allowed = key_place <= query_place
        else:
            allowed = (jnp.abs(key_place - query_place) <= WINDOW // 2) | (key_mark_ref[keys, :] + q_mark_ref[...] > 0.5)
        bias_ref[keys, :] = jnp.where(allowed, key_bias, MASKED)


def attend_forward_kernel(mode, chunks, place_ref, *refs):
    q_refs = refs[:chunks]
    near_refs = refs[chunks : 2 * chunks]
    far_refs = refs[2 * chunks : 3 * chunks]
    key_bias_ref, key_mark_ref, q_mark_ref = refs[3 * chunks : 3 * chunks + 3]
    outs = refs[3 * chunks + 3 :]
    ctx_refs, wide_refs, lse_ref, bias_ref = outs[:chunks], outs[chunks : 2 * chunks], outs[2 * chunks], outs[-1]
    cut = q_refs[0].shape[0]
    half = near_refs[0].shape[1]
    step = 256
    ones = jnp.ones((16, step), BF)
    fill_bias(mode, half // 2, place_ref, key_bias_ref, key_mark_ref, q_mark_ref, bias_ref)
    for chunk in range(chunks):
        for inner in range(cut // HD):
            feats = pl.ds(inner * HD, HD)
            value_feats = pl.ds(cut + inner * HD, HD)
            query = q_refs[chunk][feats, :]
            pieces = []
            highest = None
            for kv_ref, base in ((near_refs[chunk], 0), (far_refs[chunk], half)):
                for at in range(0, half, step):
                    keys = pl.ds(at, step)
                    scores = dot(kv_ref[feats, keys], query, 0, 0) + bias_ref[pl.ds(base + at, step), :]
                    top = jnp.max(scores, axis=0, keepdims=True)
                    highest = top if highest is None else jnp.maximum(highest, top)
                    pieces.append((scores, kv_ref, keys))
            total = None
            summed = None
            for scores, kv_ref, keys in pieces:
                lifted = jnp.exp(scores - highest)
                count = jnp.sum(lifted, axis=0, keepdims=True)
                summed = count if summed is None else summed + count
                value = jnp.concatenate([kv_ref[value_feats, keys], ones], axis=0)
                part = dot(value, lifted.astype(BF), 1, 0)
                total = part if total is None else total + part
            context = total[:HD] / total[HD : HD + 1]
            ctx_refs[chunk][feats, :] = context.astype(BF)
            wide_refs[chunk][feats, :] = context
            head = chunk * (cut // HD) + inner
            lse_ref[head : head + 1, :] = highest + jnp.log(summed)


def mask_specs(half):
    return [
        pl.BlockSpec((2 * half, 1), lambda b, p: (0, 0)),
        pl.BlockSpec((2 * half, 1), lambda b, p: (0, 0)),
        pl.BlockSpec((1, BLOCK), lambda b, p: (0, b)),
    ]


def attend_forward(mode, q, near, far, mask):
    chunks = len(q)
    cut, rows = q[0].shape
    half = near[0].shape[1]
    heads = chunks * cut // HD
    side = pl.BlockSpec((2 * cut, half), lambda b, p: (0, 0))
    lane = pl.BlockSpec((cut, BLOCK), lambda b, p: (0, b))
    out = pl.pallas_call(
        functools.partial(attend_forward_kernel, mode, chunks),
        grid_spec=pltpu.PrefetchScalarGridSpec(
            num_scalar_prefetch=1,
            grid=(rows // BLOCK,),
            in_specs=[lane] * chunks + [side] * (2 * chunks) + mask_specs(half),
            out_specs=[lane] * (2 * chunks) + [pl.BlockSpec((heads, BLOCK), lambda b, p: (0, b))],
            scratch_shapes=[pltpu.VMEM((2 * half, BLOCK), F32)],
        ),
        out_shape=[jax.ShapeDtypeStruct((cut, rows), BF)] * chunks
        + [jax.ShapeDtypeStruct((cut, rows), F32)] * chunks
        + [jax.ShapeDtypeStruct((heads, rows), F32)],
        compiler_params=pltpu.CompilerParams(vmem_limit_bytes=48 * 1024 * 1024),
        cost_estimate=pl.CostEstimate(
            flops=32 * chunks * cut * rows * half, bytes_accessed=8 * chunks * cut * half, transcendentals=0
        ),
    )(mask[0], *q, *near, *far, *mask[1:])
    return (out[:chunks], out[chunks : 2 * chunks], out[2 * chunks])


def attend_backward_kernel(mode, chunks, place_ref, *refs):
    q_refs = refs[:chunks]
    near_refs = refs[chunks : 2 * chunks]
    far_refs = refs[2 * chunks : 3 * chunks]
    key_bias_ref, key_mark_ref, q_mark_ref = refs[3 * chunks : 3 * chunks + 3]
    rest = refs[3 * chunks + 3 :]
    wide_refs, lse_ref, do_refs = rest[:chunks], rest[chunks], rest[chunks + 1 : 2 * chunks + 1]
    outs = rest[2 * chunks + 1 :]
    dq_refs, dkv_refs, sums, bias_ref = outs[:chunks], outs[chunks : 2 * chunks], outs[2 * chunks : 3 * chunks], outs[-1]
    cut = q_refs[0].shape[0]
    heads = cut // HD
    half = near_refs[0].shape[1]
    block = pl.program_id(0)
    fill_bias(mode, half // 2, place_ref, key_bias_ref, key_mark_ref, q_mark_ref, bias_ref)

    @pl.when(block == 0)
    def _():
        for total in sums:
            total[...] = jnp.zeros_like(total)

    def placed(feats, slot):
        blank = jnp.zeros_like(feats)
        pair = [feats, blank] if slot % 2 == 0 else [blank, feats]
        return jnp.concatenate(pair, axis=0).T

    for chunk in range(chunks):
        for inner in range(heads):
            feats = pl.ds(inner * HD, HD)
            value_feats = pl.ds(cut + inner * HD, HD)
            query = q_refs[chunk][feats, :]
            grad = do_refs[chunk][feats, :]
            q_side = placed(query, inner)
            do_side = placed(grad, heads + inner)
            key_lanes = pl.ds(inner // 2 * 2 * HD, 2 * HD)
            value_lanes = pl.ds((heads + inner) // 2 * 2 * HD, 2 * HD)
            head = chunk * heads + inner
            lse = lse_ref[head : head + 1, :]
            delta = jnp.sum(grad.astype(F32) * wide_refs[chunk][feats, :], axis=0, keepdims=True)
            total = None
            for kv_ref, base in ((near_refs[chunk], 0), (far_refs[chunk], half)):
                keys = pl.ds(base, half)
                scores = dot(kv_ref[feats, :], query, 0, 0) + bias_ref[keys, :]
                probs = jnp.exp(scores - lse)
                grad_probs = dot(kv_ref[value_feats, :], grad, 0, 0)
                grad_scores = (probs * (grad_probs - delta)).astype(BF)
                sums[chunk][keys, value_lanes] += dot(probs.astype(BF), do_side, 1, 0)
                sums[chunk][keys, key_lanes] += dot(grad_scores, q_side, 1, 0)
                part = dot(kv_ref[feats, :], grad_scores, 1, 0)
                total = part if total is None else total + part
            dq_refs[chunk][feats, :] = (total * (HD**-0.5)).astype(BF)

    @pl.when(block == pl.num_programs(0) - 1)
    def _():
        for chunk in range(chunks):
            dkv_refs[chunk][...] = sums[chunk][...].astype(BF)


def attend_backward(mode, q, near, far, mask, wide, lse, grad):
    chunks = len(q)
    cut, rows = q[0].shape
    half = near[0].shape[1]
    heads = chunks * cut // HD
    side = pl.BlockSpec((2 * cut, half), lambda b, p: (0, 0))
    lane = pl.BlockSpec((cut, BLOCK), lambda b, p: (0, b))
    key_side = pl.BlockSpec((2 * half, 2 * cut), lambda b, p: (0, 0))
    out = pl.pallas_call(
        functools.partial(attend_backward_kernel, mode, chunks),
        grid_spec=pltpu.PrefetchScalarGridSpec(
            num_scalar_prefetch=1,
            grid=(rows // BLOCK,),
            in_specs=[lane] * chunks
            + [side] * (2 * chunks)
            + mask_specs(half)
            + [lane] * chunks
            + [pl.BlockSpec((heads, BLOCK), lambda b, p: (0, b))]
            + [lane] * chunks,
            out_specs=[lane] * chunks + [key_side] * chunks,
            scratch_shapes=[pltpu.VMEM((2 * half, 2 * cut), F32)] * chunks + [pltpu.VMEM((2 * half, BLOCK), F32)],
        ),
        out_shape=[jax.ShapeDtypeStruct((cut, rows), BF)] * chunks
        + [jax.ShapeDtypeStruct((2 * half, 2 * cut), BF)] * chunks,
        compiler_params=pltpu.CompilerParams(vmem_limit_bytes=56 * 1024 * 1024),
        cost_estimate=pl.CostEstimate(
            flops=80 * chunks * cut * rows * half, bytes_accessed=16 * chunks * cut * half, transcendentals=0
        ),
    )(mask[0], *q, *near, *far, *mask[1:], *wide, lse, *grad)
    return (out[:chunks], out[chunks:])


def assemble_kernel(widths, at_ref, *refs):
    step = pl.program_id(0)
    slots, outs = refs[:4], refs[4:]
    for index in range(4):

        @pl.when(step == index)
        def _():
            start = 0
            for width, out in zip(widths, outs):
                out[...] = slots[index][:, start : start + width]
                start += width


def assemble(at, slots, widths):
    rows, columns = slots[0].shape
    return pl.pallas_call(
        functools.partial(assemble_kernel, widths),
        grid_spec=pltpu.PrefetchScalarGridSpec(
            num_scalar_prefetch=1,
            grid=(4,),
            in_specs=[pl.BlockSpec((rows, columns), lambda k, at: (0, 0))] * 4,
            out_specs=[pl.BlockSpec((rows, width), lambda k, at: ((at[0] + k) % 4, 0)) for width in widths],
        ),
        out_shape=[jax.ShapeDtypeStruct((4 * rows, width), BF) for width in widths],
        compiler_params=pltpu.CompilerParams(vmem_limit_bytes=40 * 1024 * 1024),
    )(at.reshape(1), *slots)


def layer_norm(z, norm):
    center = z - jnp.mean(z, axis=-1, keepdims=True)
    inverse = lax.rsqrt(jnp.mean(center * center, axis=-1, keepdims=True) + EPS)
    scaled = center * inverse
    return (scaled * norm[0] + norm[1], (scaled, inverse))


def norm_back(grad, kept, norm):
    scaled, inverse = kept
    inner = grad * norm[0]
    back = inverse * (
        inner
        - jnp.mean(inner, axis=-1, keepdims=True)
        - scaled * jnp.mean(inner * scaled, axis=-1, keepdims=True)
    )
    return (back, jnp.stack([jnp.sum(grad * scaled, axis=0), jnp.sum(grad, axis=0)]))


def gelu_both(raised):
    rise = 0.5 * (1.0 + lax.erf(raised * (0.5**0.5)))
    slope = rise + raised * jnp.exp(-0.5 * raised * raised) * 0.3989422804014327
    return ((raised * rise).astype(BF), slope.astype(BF))


def hop(value, axis, pairs):
    return lax.ppermute(value, axis, pairs)


def swap(value, axis):
    return hop(value, axis, [(0, 1), (1, 0)])


def crossing(value, to):
    pairs = [(2 * (1 - to) + y, 2 * to + 1 - y) for y in range(2)]
    return hop(value, ("section", "ty"), pairs)


def cut_gather(shard, widths, quick):
    if lax.axis_size("dp") != 4 or not quick:
        full = lax.all_gather(shard, "dp", tiled=True)
        edges = [sum(widths[:i]) for i in range(1, len(widths))]
        return jnp.split(full, edges, axis=1)
    at = lax.axis_index("dp")
    up = hop(shard, "dp", [(j, (j - 1) % 4) for j in range(4)])
    down = hop(shard, "dp", [(j, (j + 1) % 4) for j in range(4)])
    from_up = hop(up, "dp", [(1, 0), (2, 1)])
    from_down = hop(down, "dp", [(1, 2), (2, 3)])
    far = jnp.where(at < 2, from_up, from_down)
    return assemble(at, (shard, up, far, down), widths)


def cut_scatter(tensors, quick):
    size = lax.axis_size("dp")
    if size != 4 or not quick:
        full = jnp.concatenate(tensors, axis=1)
        return lax.psum_scatter(full, "dp", tiled=True).astype(F32)
    at = lax.axis_index("dp")
    rows = tensors[0].shape[0] // 4

    def slot(k):
        start = lax.rem(at + k, 4) * rows
        return jnp.concatenate([lax.dynamic_slice_in_dim(t, start, rows, 0) for t in tensors], axis=1)

    far = slot(2)
    to_up = hop(far, "dp", [(0, 1), (1, 2)])
    to_down = hop(far, "dp", [(2, 1), (3, 2)])
    ahead = add_low(slot(1), to_up)
    behind = add_low(slot(3), to_down)
    from_behind = hop(ahead, "dp", [(j, (j + 1) % 4) for j in range(4)])
    from_ahead = hop(behind, "dp", [(j, (j - 1) % 4) for j in range(4)])
    return slot(0).astype(F32) + from_behind.astype(F32) + from_ahead.astype(F32)


def add_low(a, b):
    return (a.astype(F32) + b.astype(F32)).astype(BF)


def everywhere(value):
    for axis in ("tc", "ty", "section"):
        value = value + swap(value, axis)
    size = lax.axis_size("dp")
    reach = 1
    while reach < size:
        value = value + hop(value, "dp", [(j, j ^ reach) for j in range(size)])
        reach *= 2
    return value


def tie(value, token):
    first = token[(0,) * token.ndim]
    return jnp.where(first == first, value, jnp.zeros_like(value))


def total_of(parts):
    total = parts[0]
    for part in parts[1:]:
        total = total + part
    return total


def local(source, target, src_len, tgt_len, global_mask, attn_w, proj_w, cross_w, up_w, down_w, norms, dec_cot):
    section = lax.axis_index("section")
    y = lax.axis_index("ty")
    c = lax.axis_index("tc")
    src_rows = source.shape[1]
    tgt_rows = target.shape[1]
    width = source.shape[2]
    src_own = src_rows // 4
    tgt_own = tgt_rows // 4
    cut = attn_w.shape[1]
    heads = attn_w.shape[3]
    units = up_w.shape[2]
    scale = HD**-0.5

    def pick(array):
        return lax.dynamic_index_in_dim(array, section, 0, keepdims=False)

    src_length = pick(src_len)
    tgt_length = pick(tgt_len)
    order = jnp.stack([2 * y + c, 2 * y + 1 - c, 2 * (1 - y) + c, 2 * (1 - y) + 1 - c]).astype(jnp.int32)

    def ordered(array):
        size = array.shape[0] // 4
        return jnp.concatenate([lax.dynamic_slice_in_dim(array, order[i] * size, size, 0) for i in range(4)])

    src_place = ordered(jnp.arange(src_rows, dtype=jnp.int32))
    tgt_place = ordered(jnp.arange(tgt_rows, dtype=jnp.int32))
    src_valid = (src_place[:src_own] < src_length).astype(F32)[:, None]
    tgt_valid = (tgt_place[:tgt_own] < tgt_length).astype(F32)[:, None]
    marks = ordered(pick(global_mask) > 0).astype(F32)
    src_bias = jnp.where(src_place < src_length, 0.0, MASKED).astype(F32)[:, None]
    tgt_bias = jnp.where(tgt_place < tgt_length, 0.0, MASKED).astype(F32)[:, None]

    def places(place, queries):
        size = place.shape[0] // 4
        return jnp.concatenate([place[::size], queries[::BLOCK]])

    src_chip = 2 * src_own
    tgt_chip = 2 * tgt_own
    enc_mask = (places(src_place, src_place[:src_chip]), src_bias, marks[:, None], marks[None, :src_chip])
    dec_mask = (places(tgt_place, tgt_place[:tgt_chip]), tgt_bias, tgt_bias, tgt_bias[:tgt_chip].T)
    cross_mask = (places(src_place, tgt_place[:tgt_chip]), src_bias, src_bias, dec_mask[3])

    flat = attn_w.reshape(cut, 3 * heads)
    kv_cut = flat[:, heads:]
    qp_cut = jnp.concatenate([flat[:, :heads], proj_w[0].T], axis=1)
    up_cut = up_w.reshape(cut, units)
    down_cut = down_w[0].T
    cross_cut = cross_w.reshape(cut, 2 * heads)

    cuts = {"kv": kv_cut, "qp": qp_cut, "up": up_cut, "down": down_cut, "cross": cross_cut}
    sizes = {name: value.shape[1] for name, value in cuts.items()}

    def packed(names):
        return jnp.concatenate([cuts[name] for name in names], axis=1)

    def spread(layer, names, full):
        chunks = {}
        for name, mine in zip(names, full):
            by_x = name in ("kv", "up") or (name == "cross" and layer == 0)
            chunks[name] = [mine, swap(mine, "section" if by_x else "ty")]
        return chunks

    norms_all = jnp.stack([norms[0], swap(norms[0], "section")])
    norms_all = jnp.where(section == 0, norms_all, norms_all[::-1])
    norm_e = norms_all[0]
    norm_d = norms_all[1]

    attn_names, feed_names = ("kv", "qp"), ("up", "down")
    attn_width = sizes["kv"] + sizes["qp"]
    feed_width = sizes["up"] + sizes["down"]
    everything = packed(attn_names + feed_names + ("cross",))
    came = hop(everything, ("section", "ty"), [(2 * x + v, 2 * (1 - x) + 1 - v) for x in range(2) for v in range(2)])
    all_e = jnp.where(section == 0, everything, came)
    all_d = jnp.where(section == 1, everything, came)

    full = cut_gather(all_e[:, :attn_width], [sizes[name] for name in attn_names], True)
    w_e = spread(0, attn_names, full)
    shard = all_e[:, attn_width : attn_width + feed_width]
    w_e.update(spread(0, feed_names, cut_gather(shard, [sizes[name] for name in feed_names], False)))
    token = w_e["up"][0]
    shard = jnp.concatenate([all_e[:, attn_width + feed_width :], all_d[:, :attn_width]], axis=1)
    full = cut_gather(tie(shard, token), [sizes["cross"], sizes["kv"], sizes["qp"]], False)
    w_e.update(spread(0, ("cross",), full[:1]))
    w_d = spread(1, attn_names, full[1:])
    token = w_d["kv"][0]
    names = ("cross",) + feed_names
    shard = jnp.concatenate([all_d[:, attn_width + feed_width :], all_d[:, attn_width : attn_width + feed_width]], axis=1)
    w_d.update(spread(1, names, cut_gather(tie(shard, token), [sizes[name] for name in names], False)))

    both = range(2)

    def key_values(weights, rows):
        return [dot(weights[r], rows, 0, 1).astype(BF) for r in both]

    def queries(weights, rows):
        return [(dot(weights[r][:, :heads], rows, 0, 1) * scale).astype(BF) for r in both]

    def chip(rows):
        return jnp.concatenate([rows, swap(rows, "tc")])

    def own_sum(partial_rows):
        mine = partial_rows.shape[0] // 2
        return partial_rows[:mine] + swap(partial_rows[mine:].astype(BF), "tc").astype(F32)

    def feed_forward(low, up, down):
        active, slope, parts = [], [], []
        for r in both:
            act, rise = gelu_both(dot(low, up[r], 1, 0))
            active.append(act)
            slope.append(rise)
            parts.append(dot(act, down[r], 1, 1))
        return (active, slope, own_sum(total_of(parts)))

    def chip_total(partial_of, by_x):
        other = swap(partial_of(1).astype(BF), "section" if by_x else "ty")

        def finish(token):
            return (partial_of(0) + tie(other, token).astype(F32)).astype(BF)

        return finish

    def feed_back(low, active, slope, lowered_grad, up, down):
        raised = []
        for r in both:
            grad_active = dot(lowered_grad, down[r], 1, 0)
            raised.append((grad_active * slope[r].astype(F32)).astype(BF))
        back = own_sum(total_of([dot(raised[r], up[r], 1, 1) for r in both]))
        grad_up = chip_total(lambda r: dot(low, raised[r], 0, 0), True)
        grad_down = chip_total(lambda r: dot(lowered_grad, active[r], 0, 0), False)
        return (back, grad_up, grad_down)

    def project(ctx, weights, start):
        return total_of([dot(ctx[r], weights[r][:, start : start + heads], 0, 1) for r in both])

    def project_back(rows, weights, start):
        return [dot(weights[r][:, start : start + heads], rows, 0, 1).astype(BF) for r in both]

    def all_rows(weights, grads, more):
        partial_rows = total_of([dot(grads[r], weights[r], 1, 1) for r in both])
        size = partial_rows.shape[0] // 4
        parts = [partial_rows[i * size : (i + 1) * size] for i in range(4)]
        if more is not None:
            parts = [parts[0] + more[:size], parts[1] + more[size:], parts[2], parts[3]]
        from_core = swap(jnp.concatenate([parts[1], parts[3]]).astype(BF), "tc").astype(F32)
        leaving = (parts[2] + from_core[size:]).astype(BF)
        return (parts[0] + from_core[:size], swap(leaving, "ty"), leaving)

    normed, kept = layer_norm(ordered(pick(source)).astype(F32), norm_e[0])
    enc_kept_zero = (kept[0][:src_own], kept[1][:src_own])
    normed_low = normed.astype(BF)
    normed_mine = normed[:src_own]
    low_chip = normed_low[:src_chip]
    enc_near = key_values(w_e["kv"], low_chip)
    enc_far = key_values(w_e["kv"], normed_low[src_chip:])
    enc_q = queries(w_e["qp"], low_chip)
    enc_ctx, enc_wide, enc_lse = attend_forward("window", enc_q, enc_near, enc_far, enc_mask)
    middle, enc_kept_one = layer_norm(normed_mine + own_sum(project(enc_ctx, w_e["qp"], heads)), norm_e[1])
    middle_low = chip(middle.astype(BF))
    enc_active, enc_slope, lowered = feed_forward(middle_low, w_e["up"], w_e["down"])
    memory, enc_kept_two = layer_norm(middle + lowered, norm_e[2])
    memory_low = (memory * src_valid).astype(BF)
    memory_near = chip(memory_low)
    memory_far = chip(swap(memory_low, "ty"))
    mem_near = key_values(w_e["cross"], memory_near)
    mem_far = key_values(w_e["cross"], memory_far)

    tgt_low = ordered(pick(target))
    tgt_low_chip = tgt_low[:tgt_chip]
    dec_near = key_values(w_d["kv"], tgt_low_chip)
    dec_far = key_values(w_d["kv"], tgt_low[tgt_chip:])
    dec_q = queries(w_d["qp"], tgt_low_chip)
    dec_ctx, dec_wide, dec_lse = attend_forward("causal", dec_q, dec_near, dec_far, dec_mask)
    first, dec_kept_zero = layer_norm(
        tgt_low[:tgt_own].astype(F32) + own_sum(project(dec_ctx, w_d["qp"], heads)), norm_d[0]
    )
    first_low = chip(first.astype(BF))
    asking = queries(w_d["cross"], first_low)
    mem_near, mem_far = (mem_near[::-1], mem_far[::-1])
    crossed, cross_wide, cross_lse = attend_forward("all", asking, mem_near, mem_far, cross_mask)
    second, dec_kept_one = layer_norm(first + own_sum(project(crossed, w_d["cross"], heads)), norm_d[1])
    second_low = chip(second.astype(BF))
    dec_active, dec_slope, lowered = feed_forward(second_low, w_d["up"], w_d["down"])
    result, dec_kept_two = layer_norm(second + lowered, norm_d[2])
    output = (result * tgt_valid).astype(BF)

    cotangent = lax.dynamic_slice_in_dim(pick(dec_cot), order[0] * tgt_own, tgt_own, 0).astype(F32) * tgt_valid
    back_two, dnorm_d2 = norm_back(cotangent, dec_kept_two, norm_d[2])
    back, grad_up_d, grad_down_d = feed_back(
        second_low, dec_active, dec_slope, chip(back_two.astype(BF)), w_d["up"], w_d["down"]
    )
    back_one, dnorm_d1 = norm_back(back_two + back, dec_kept_one, norm_d[1])
    answer_grad = chip(back_one.astype(BF))
    crossed_grad = project_back(answer_grad, w_d["cross"], heads)
    asking_grad, mem_grad = attend_backward(
        "all", asking, mem_near, mem_far, cross_mask, cross_wide, cross_lse, crossed_grad
    )
    mem_grad = mem_grad[::-1]
    memory_mine, memory_other, leaving = all_rows(w_e["cross"], mem_grad, None)

    def two_sided(left, left_grad, right, right_grad):
        return lambda r: jnp.concatenate([dot(left, left_grad[r], 0, 1), dot(right, right_grad[r], 0, 1)], axis=1)

    grad_cross_d = chip_total(two_sided(first_low, asking_grad, answer_grad, crossed), False)
    memory_set = jnp.concatenate([memory_near, memory_far])
    grad_cross_e = chip_total(lambda r: dot(memory_set, mem_grad[r], 0, 0), True)
    back_zero, dnorm_d0 = norm_back(
        back_one + own_sum(project(asking_grad, w_d["cross"], 0)), dec_kept_zero, norm_d[0]
    )
    mixed_grad = chip(tie(back_zero, leaving).astype(BF))
    ctx_grad = project_back(mixed_grad, w_d["qp"], heads)
    dec_dq, dec_dkv = attend_backward("causal", dec_q, dec_near, dec_far, dec_mask, dec_wide, dec_lse, ctx_grad)
    target_mine, target_other, leaving = all_rows(w_d["kv"], dec_dkv, project(dec_dq, w_d["qp"], 0))
    grad_qp_d = chip_total(two_sided(tgt_low_chip, dec_dq, mixed_grad, dec_ctx), False)
    grad_kv_d = chip_total(lambda r: dot(tgt_low, dec_dkv[r], 0, 0), True)

    memory_grad = memory_mine + tie(memory_other, dec_dq[0]).astype(F32)
    back_two, dnorm_e2 = norm_back(memory_grad * src_valid, enc_kept_two, norm_e[2])
    back, grad_up_e, grad_down_e = feed_back(
        middle_low, enc_active, enc_slope, chip(back_two.astype(BF)), w_e["up"], w_e["down"]
    )
    back_one, dnorm_e1 = norm_back(back_two + back, enc_kept_one, norm_e[1])
    mixed_grad = chip(back_one.astype(BF))
    ctx_grad = project_back(mixed_grad, w_e["qp"], heads)
    enc_dq, enc_dkv = attend_backward("window", enc_q, enc_near, enc_far, enc_mask, enc_wide, enc_lse, ctx_grad)
    target_grad = (back_zero + target_mine + tie(target_other, enc_dq[0]).astype(F32)).astype(BF)
    normed_mine, normed_other, leaving = all_rows(w_e["kv"], enc_dkv, project(enc_dq, w_e["qp"], 0))
    grad_qp_e = chip_total(two_sided(low_chip, enc_dq, mixed_grad, enc_ctx), False)
    grad_kv_e = chip_total(lambda r: dot(normed_low, enc_dkv[r], 0, 0), True)

    grad_up_d, grad_down_d = (grad_up_d(asking_grad[0]), grad_down_d(asking_grad[0]))
    grad_cross_d = grad_cross_d(dec_dq[0])
    grad_cross_e = grad_cross_e(dec_dq[0])
    grad_qp_d, grad_kv_d = (grad_qp_d(back_two), grad_kv_d(back_two))
    grad_up_e, grad_down_e = (grad_up_e(enc_dq[0]), grad_down_e(enc_dq[0]))
    grad_qp_e, grad_kv_e = (grad_qp_e(leaving), grad_kv_e(leaving))
    normed_grad = normed_mine + tie(normed_other, grad_kv_e).astype(F32)
    back_zero, dnorm_e0 = norm_back(back_one + normed_grad, enc_kept_zero, norm_e[0])
    source_grad = back_zero.astype(BF)

    dec_feed = cut_scatter([grad_up_d, grad_down_d], False)
    dec_rest = cut_scatter([grad_cross_d, grad_kv_d, grad_qp_d], False)
    dec_sum = jnp.concatenate([dec_rest, dec_feed], axis=1)
    dec_sum = dec_sum + crossing(dec_sum.astype(BF), 1).astype(F32)
    enc_feed = cut_scatter([grad_cross_e, grad_up_e, grad_down_e], False)
    enc_attn = cut_scatter([grad_kv_e, grad_qp_e], True)
    enc_feed = enc_feed + crossing(enc_feed.astype(BF), 0).astype(F32)
    enc_attn = enc_attn + crossing(enc_attn.astype(BF), 0).astype(F32)
    cross_width = sizes["cross"]
    cross = jnp.where(section == 0, enc_feed[:, :cross_width], dec_sum[:, :cross_width])
    attn = jnp.where(section == 0, enc_attn, dec_sum[:, cross_width : cross_width + attn_width])
    feed = jnp.where(section == 0, enc_feed[:, cross_width:], dec_sum[:, cross_width + attn_width :])
    norm_sum = everywhere(
        jnp.stack([jnp.stack([dnorm_e0, dnorm_e1, dnorm_e2]), jnp.stack([dnorm_d0, dnorm_d1, dnorm_d2])])
    )
    norm_share = lax.dynamic_slice(norm_sum, (section, 0, 0, lax.axis_index("dp") * cut), (1, 3, 2, cut))

    def everyone(rows):
        full = lax.all_gather(rows, ("section", "ty", "tc"), tiled=True)
        return full.reshape(2, -1, width)

    grad_attn = jnp.concatenate([attn[:, 2 * heads : 3 * heads], attn[:, : 2 * heads]], axis=1)
    return (
        everyone(output),
        everyone(source_grad),
        everyone(target_grad),
        grad_attn.reshape(1, cut, 3, heads),
        attn[:, 3 * heads :].T[None],
        cross.reshape(1, cut, 2, heads),
        feed[None, :, :units],
        feed[:, units:].T[None],
        norm_share,
    )


def solution(mesh):
    shape = mesh.devices.shape
    fine = Mesh(mesh.devices.reshape(shape[0], shape[1], 2, 2), ("section", "dp", "ty", "tc"))
    tensor = ("ty", "tc")
    return jax.shard_map(
        local,
        mesh=fine,
        in_specs=(
            P("dp", None, None),
            P("dp", None, None),
            P("dp"),
            P("dp"),
            P("dp", None),
            P("section", "dp", None, tensor),
            P("section", tensor, "dp"),
            P("section", "dp", None, tensor),
            P("section", "dp", tensor),
            P("section", tensor, "dp"),
            P("section", None, None, None),
            P("dp", None, None),
        ),
        out_specs=(
            P("dp", None, None),
            P("dp", None, None),
            P("dp", None, None),
            P("section", "dp", None, tensor),
            P("section", tensor, "dp"),
            P("section", "dp", None, tensor),
            P("section", "dp", tensor),
            P("section", tensor, "dp"),
            P("section", None, None, "dp"),
        ),
        check_vma=False,
    )
```

time: 1120 us -> 734 us (0.66)
  waiting for transfers between devices: 576 us -> 181 us
  local copies, waits for them, and re-layouts: 164 us -> 94.7 us
  starting transfers between devices: 7 us -> 66.1 us
  blocking collectives: 44.9 us -> 0 us
  matrix products: 115 us -> 143 us
  Pallas kernels: 113 us -> 127 us
  between operations: 17 us -> 29.5 us
    reduce_scatter x3 -> x1, waiting for transfers between devices: 334 us -> 0.01 us  [cut_scatter(): return lax.psum_scatter(full, 'dp', tiled=True).astype(F32)]
    all_gather x3, waiting for transfers between devices: 191 us -> 12.3 us  [cut_gather(): full = lax.all_gather(shard, 'dp', tiled=True)]
    ppermute x10 -> x63, waiting for transfers between devices: 50.8 us -> 168 us  [hop(): return lax.ppermute(value, axis, pairs)]
    ppermute x10 -> x63, starting transfers between devices: 6.16 us -> 65.2 us  [hop(): return lax.ppermute(value, axis, pairs)]
    another operation x3 -> x0, local copies, waits for them, and re-layouts: 44.1 us -> none  [scatter(): both = jnp.stack([enc, dec]).astype(BF).reshape(-1, enc.shape[2])]
    slice x27 -> x34, local copies, waits for them, and re-layouts: 57.2 us -> 13.6 us  [the longest x9 7.34 us: tie(): first = token[(0,) * token.ndim]]
    psum x1 -> x0, blocking collectives: 39.6 us -> none  [local(): lax.psum(jnp.stack([jnp.stack([dnorm_e0, dnorm_e1, dnorm_e2]), jnp.stack(...]
    dot_general x44 -> x84, matrix products: 111 us -> 143 us  [dot(): lax.dot_general(a, b, (((ca,), (cb,)), ((), ())), preferred_element_type=...]
  transfers between devices with their start and end apart: 19 -> 72, of which waited for: 9 -> 29; matrix products, arithmetic and copies ran while one was open for 25% -> 38% of each run, Pallas kernels for 7% -> 16%
where the time goes in v2:
time: 734 us; the launch traced here: 721 us
  waiting for transfers between devices  181 us (25%)
  matrix products  143 us (19%)
  Pallas kernels  127 us (17%)
  local copies, waits for them, and re-layouts  94.7 us (13%)
  other arithmetic  79.9 us (11%)
  starting transfers between devices  66.1 us (9%)
  between operations  29.5 us (4%)
    ppermute x63, waiting for transfers between devices, hop(): return lax.ppermute(value, axis, pairs)  168 us
    dot_general x84, matrix products, dot(): lax.dot_general(a, b, (((ca,), (cb,)), ((), ())), preferred_element_type=...  143 us
    pallas_call x3, Pallas kernels, attend_backward(): pl.pallas_call(functools.partial(attend_backward_kernel, mode, chunks), g...  77.8 us
    ppermute x63, starting transfers between devices, hop(): return lax.ppermute(value, axis, pairs)  65.2 us
    unnamed x454, local copies, waits for them, and re-layouts  49.4 us
    pallas_call x3, Pallas kernels, attend_forward(): pl.pallas_call(functools.partial(attend_forward_kernel, mode, chunks), gr...  49 us
  transfers between devices with their start and end apart: 72, of which 29 were waited for; matrix products, arithmetic and copies ran while one was open for 38% of the time, Pallas kernels for 16%

profile of v2, /device:TPU:0, one launch (start us, length us, event | category | flops | bytes accessed | tf_op | source)
XLA Modules:
  0.0 721.0 jit_solution(10522969712402546053)
XLA Ops:
  34.0 5.6 collective-permute-done
  46.6 7.2 %collective-permute-done.10.refs_3_ = bf16[192,768]{1,0:T(8,128)(2,1)S(1)} collective-permute-done((bf16[192,768]{1,0:T(8,128)(2,1)S(1)}, bf16[192,768]{1,0:T(8,128)(2,1)S(1)}, u32[]{:S(2)}, u32[]{:S(2)}) %collective-permute-start.10) | collective-permute-done | bytes 294944 | tf_op jit(solution)/shard_map/ppermute | solution.py:259
  58.6 7.2 fusion.164
  75.2 7.6 %collective-permute-done.13 = bf16[768,384]{1,0:T(8,128)(2,1)S(1)} collective-permute-done((bf16[768,384]{1,0:T(8,128)(2,1)S(1)}, bf16[768,384]{1,0:T(8,128)(2,1)S(1)}, u32[]{:S(2)}, u32[]{:S(2)}) %collective-permute-start.13) | collective-permute-done | bytes 589856 | tf_op jit(solution)/shard_map/ppermute | solution.py:259
  86.2 28.6 %shard_map.189 = (bf16[192,1024]{1,0:T(8,128)(2,1)S(1)}, bf16[192,1024]{1,0:T(8,128)(2,1)S(1)}, f32[192,1024]{1,0:T(8,128)S(1)}, f32[192,1024]{1,0:T(8,128)S(1)}, f32[6,1024]{1,0:T(8,128)S(1)}) custom-call(s32[8]{0:T(128)S(1)} %pad_add_fusion.7.place_ref, bf16[192,1024]{1,0:T(8,128)(2,1)S(1)} %fusion.37.refs_0_, bf16[192,1024]{1,0:T(8,128)(2,1)S(1)} %fusion.38.refs_1_, ...), custom_call_target="tpu_custom_call" | custom-call | flops 12884901888 | bytes 3145728 | tf_op jit(solution)/shard_map/pallas_call | solution.py:97
  133.1 4.8 multiply_convert_fusion.3
  138.0 17.1 %collective-permute-done.16 = bf16[768,768]{1,0:T(8,128)(2,1)} collective-permute-done((bf16[768,768]{1,0:T(8,128)(2,1)}, bf16[768,768]{1,0:T(8,128)(2,1)}, u32[]{:S(2)}, u32[]{:S(2)}) %collective-permute-start.16) | collective-permute-done | bytes 1179680 | tf_op jit(solution)/shard_map/ppermute | solution.py:259
  155.1 4.9 multiply_convert_fusion.2
  190.8 9.4 %collective-permute-done.20 = bf16[512,768]{1,0:T(8,128)(2,1)S(1)} collective-permute-done((bf16[512,768]{1,0:T(8,128)(2,1)}, bf16[512,768]{1,0:T(8,128)(2,1)S(1)}, u32[]{:S(2)}, u32[]{:S(2)}) %collective-permute-start.20) | collective-permute-done | bytes 786464 | tf_op jit(solution)/shard_map/ppermute | solution.py:259
  203.6 8.0 %collective-permute-done.1 = bf16[768,384]{1,0:T(8,128)(2,1)S(1)} collective-permute-done((bf16[768,384]{1,0:T(8,128)(2,1)S(1)}, bf16[768,384]{1,0:T(8,128)(2,1)S(1)}, u32[]{:S(2)}, u32[]{:S(2)}) %collective-permute-start.1) | collective-permute-done | bytes 589856 | tf_op jit(solution)/shard_map/ppermute | solution.py:259
  216.2 7.7 %shard_map.187 = (bf16[192,512]{1,0:T(8,128)(2,1)S(1)}, bf16[192,512]{1,0:T(8,128)(2,1)S(1)}, f32[192,512]{1,0:T(8,128)S(1)}, f32[192,512]{1,0:T(8,128)S(1)}, f32[6,512]{1,0:T(8,128)S(1)}) custom-call(s32[6]{0:T(128)S(1)} %get-tuple-element.214.place_ref, bf16[192,512]{1,0:T(8,128)(2,1)S(1)} %fusion.42.refs_0_, bf16[192,512]{1,0:T(8,128)(2,1)S(1)} %fusion.43.refs_1_, ...), custom_call_target="tpu_custom_call" | custom-call | flops 3221225472 | bytes 1572864 | tf_op jit(solution)/shard_map/pallas_call | solution.py:97
  232.0 12.3 %all-gather.11.cloned.1.call-done = bf16[768,1920]{1,0:T(8,128)(2,1)} async-done(((bf16[192,1920]{1,0:T(8,128)(2,1)}), bf16[768,1920]{1,0:T(8,128)(2,1)}) %all-gather.11.cloned.1.call-update) | async-done | bytes 2949136 | tf_op jit(solution)/shard_map/all_gather | solution.py:273
  253.3 7.2 %collective-permute-done.6 = bf16[768,384]{1,0:T(8,128)(2,1)S(1)} collective-permute-done((bf16[768,384]{1,0:T(8,128)(2,1)S(1)}, bf16[768,384]{1,0:T(8,128)(2,1)S(1)}, u32[]{:S(2)}, u32[]{:S(2)}) %collective-permute-start.6) | collective-permute-done | bytes 589856 | tf_op jit(solution)/shard_map/ppermute | solution.py:259
  262.4 12.7 %shard_map.190 = (bf16[192,512]{1,0:T(8,128)(2,1)S(1)}, bf16[192,512]{1,0:T(8,128)(2,1)S(1)}, f32[192,512]{1,0:T(8,128)S(1)}, f32[192,512]{1,0:T(8,128)S(1)}, f32[6,512]{1,0:T(8,128)S(1)}) custom-call(s32[6]{0:T(128)S(1)} %get-tuple-element.215.place_ref, bf16[192,512]{1,0:T(8,128)(2,1)S(1)} %fusion.44.refs_0_, bf16[192,512]{1,0:T(8,128)(2,1)S(1)} %fusion.45.refs_1_, ...), custom_call_target="tpu_custom_call" | custom-call | flops 6442450944 | bytes 3145728 | tf_op jit(solution)/shard_map/pallas_call | solution.py:97
  281.6 23.4 %collective-permute-done.24 = bf16[768,768]{1,0:T(8,128)(2,1)S(1)} collective-permute-done((bf16[768,768]{1,0:T(8,128)(2,1)S(1)}, bf16[768,768]{1,0:T(8,128)(2,1)S(1)}, u32[]{:S(2)}, u32[]{:S(2)}) %collective-permute-start.24) | collective-permute-done | bytes 1179680 | tf_op jit(solution)/shard_map/ppermute | solution.py:259
  338.8 22.8 %shard_map.191 = (bf16[192,512]{1,0:T(8,128)(2,1)}, bf16[192,512]{1,0:T(8,128)(2,1)}, bf16[2048,384]{1,0:T(8,128)(2,1)}, bf16[2048,384]{1,0:T(8,128)(2,1)}) custom-call(s32[6]{0:T(128)} %copy-done.13, bf16[192,512]{1,0:T(8,128)(2,1)} %copy-done.28, bf16[192,512]{1,0:T(8,128)(2,1)} %copy-done.29, bf16[384,1024]{1,0:T(8,128)(2,1)} %convolution_convert_fusion.7.refs_2_, ...), custom_call_target="tpu_custom_call" | custom-call | flops 16106127360 | bytes 6291456 | tf_op jit(solution)/shard_map/pallas_call | solution.py:182
  405.3 13.8 %shard_map.192 = (bf16[192,512]{1,0:T(8,128)(2,1)}, bf16[192,512]{1,0:T(8,128)(2,1)}, bf16[1024,384]{1,0:T(8,128)(2,1)}, bf16[1024,384]{1,0:T(8,128)(2,1)}) custom-call(s32[6]{0:T(128)} %copy-done.12, bf16[192,512]{1,0:T(8,128)(2,1)} %copy-done.26, bf16[192,512]{1,0:T(8,128)(2,1)} %copy-done.27, bf16[384,512]{1,0:T(8,128)(2,1)} %copy-done.25, ...), custom_call_target="tpu_custom_call" | custom-call | flops 8053063680 | bytes 3145728 | tf_op jit(solution)/shard_map/pallas_call | solution.py:182
  477.4 41.1 %shard_map.193 = (bf16[192,1024]{1,0:T(8,128)(2,1)}, bf16[192,1024]{1,0:T(8,128)(2,1)}, bf16[2048,384]{1,0:T(8,128)(2,1)}, bf16[2048,384]{1,0:T(8,128)(2,1)}) custom-call(s32[8]{0:T(128)} %copy-done.14, bf16[192,1024]{1,0:T(8,128)(2,1)} %copy-done.22, bf16[192,1024]{1,0:T(8,128)(2,1)} %copy-done.23, bf16[384,1024]{1,0:T(8,128)(2,1)} %copy-done.17, ...), custom_call_target="tpu_custom_call" | custom-call | flops 32212254720 | bytes 6291456 | tf_op jit(solution)/shard_map/pallas_call | solution.py:182
  539.6 10.1 %collective-permute-done.41 = bf16[256,768]{1,0:T(8,128)(2,1)S(1)} collective-permute-done((bf16[256,768]{1,0:T(8,128)(2,1)S(1)}, bf16[256,768]{1,0:T(8,128)(2,1)S(1)}, u32[]{:S(2)}, u32[]{:S(2)}) %collective-permute-start.41) | collective-permute-done | bytes 393248 | tf_op jit(solution)/shard_map/ppermute | solution.py:259
  566.5 10.1 %collective-permute-done.38 = bf16[768,384]{0,1:T(8,128)(2,1)S(1)} collective-permute-done((bf16[768,384]{0,1:T(8,128)(2,1)S(1)}, bf16[768,384]{0,1:T(8,128)(2,1)S(1)}, u32[]{:S(2)}, u32[]{:S(2)}) %collective-permute-start.38) | collective-permute-done | bytes 589856 | tf_op jit(solution)/shard_map/ppermute | solution.py:259
  602.1 9.3 %collective-permute-done.42 = bf16[768,384]{0,1:T(8,128)(2,1)} collective-permute-done((bf16[768,384]{0,1:T(8,128)(2,1)}, bf16[768,384]{0,1:T(8,128)(2,1)}, u32[]{:S(2)}, u32[]{:S(2)}) %collective-permute-start.42) | collective-permute-done | bytes 589856 | tf_op jit(solution)/shard_map/ppermute | solution.py:259
  632.1 4.9 collective-permute-done.46
  637.0 5.9 collective-permute-done.44
  673.7 16.1 %collective-permute-done.57 = bf16[192,1920]{1,0:T(8,128)(2,1)} collective-permute-done((bf16[192,1920]{1,0:T(8,128)(2,1)}, bf16[192,1920]{1,0:T(8,128)(2,1)}, u32[]{:S(2)}, u32[]{:S(2)}) %collective-permute-start.57) | collective-permute-done | bytes 737312 | tf_op jit(solution)/shard_map/ppermute | solution.py:259
  (877 shorter events, 393.8 us)
Async XLA Ops:
  7.2 116.1 %all-gather.7.cloned.1.call-start = ((), (), s32[]{:S(2)}) async-start(), calls=%async_computation.3 | async-start | bytes 2949120 | tf_op jit(solution)/shard_map/all_gather | solution.py:273
  66.6 114.4 %all-gather.9.cloned.1.call-start = ((), (), s32[]{:S(2)}) async-start(), calls=%async_computation.4 | async-start | bytes 2211840 | tf_op jit(solution)/shard_map/all_gather | solution.py:273
  126.6 28.5 %collective-permute-start.16 = (bf16[768,768]{1,0:T(8,128)(2,1)}, bf16[768,768]{1,0:T(8,128)(2,1)}, u32[]{:S(2)}, u32[]{:S(2)}) collective-permute-start(bf16[768,768]{1,0:T(8,128)(2,1)} %get-tuple-element.191), channel_id=1, source_target_pairs={{0,16},{16,0},{1,17},{17,1},{2,18},{18,2},{3,19},{19,3},{4,20},{20... | collective-permute-start | bytes 3538952 | tf_op jit(solution)/shard_map/ppermute | solution.py:259
  127.1 32.9 %collective-permute-start.17 = (bf16[768,768]{1,0:T(8,128)(2,1)}, bf16[768,768]{1,0:T(8,128)(2,1)}, u32[]{:S(2)}, u32[]{:S(2)}) collective-permute-start(bf16[768,768]{1,0:T(8,128)(2,1)} %get-tuple-element.190), channel_id=1, source_target_pairs={{0,2},{2,0},{1,3},{3,1},{4,6},{6,4},{5,7},{7,5},{8,10},{10,8},{9,1... | collective-permute-start | bytes 3538952 | tf_op jit(solution)/shard_map/ppermute | solution.py:259
  133.1 111.2 %all-gather.11.cloned.1.call-start = ((), (), s32[]{:S(2)}) async-start(), calls=%async_computation.5 | async-start | bytes 3686400 | tf_op jit(solution)/shard_map/all_gather | solution.py:273
  184.6 413.6 %all-gather.13.cloned.1.call-start = ((), (), s32[]{:S(2)}) async-start(), calls=%async_computation.6 | async-start | bytes 3538944 | tf_op jit(solution)/shard_map/all_gather | solution.py:592
  186.6 38.7 %collective-permute-start.7 = (bf16[768,384]{1,0:T(8,128)(2,1)S(1)}, bf16[768,384]{1,0:T(8,128)(2,1)S(1)}, u32[]{:S(2)}, u32[]{:S(2)}) collective-permute-start(bf16[768,384]{1,0:T(8,128)(2,1)S(1)} %get-tuple-element.194), channel_id=1, source_target_pairs={{0,16},{16,0},{1,17},{17,1},{2,18},{18,2},{3,19},{19,3},{4,20},{20... | collective-permute-start | bytes 1769480 | tf_op jit(solution)/shard_map/ppermute | solution.py:259
  200.1 28.5 %collective-permute-start.21 = (bf16[512,768]{1,0:T(8,128)(2,1)S(1)}, bf16[512,768]{1,0:T(8,128)(2,1)S(1)}, u32[]{:S(2)}, u32[]{:S(2)}) collective-permute-start(bf16[512,768]{1,0:T(8,128)(2,1)S(1)} %collective-permute-done.20), channel_id=1, source_target_pairs={{0,1},{1,0},{2,3},{3,2},{4,5},{5,4},{6,7},{7,6},{8,9},{9,8},{10,11... | collective-permute-start | bytes 2359304 | tf_op jit(solution)/shard_map/ppermute | solution.py:259
  276.6 28.4 %collective-permute-start.24 = (bf16[768,768]{1,0:T(8,128)(2,1)S(1)}, bf16[768,768]{1,0:T(8,128)(2,1)S(1)}, u32[]{:S(2)}, u32[]{:S(2)}) collective-permute-start(bf16[768,768]{1,0:T(8,128)(2,1)S(1)} %get-tuple-element.189), channel_id=1, source_target_pairs={{0,16},{16,0},{1,17},{17,1},{2,18},{18,2},{3,19},{19,3},{4,20},{20... | collective-permute-start | bytes 3538952 | tf_op jit(solution)/shard_map/ppermute | solution.py:259
  328.3 65.4 %collective-permute-start.51 = (bf16[768,768]{0,1:T(8,128)(2,1)}, bf16[768,768]{0,1:T(8,128)(2,1)}, u32[]{:S(2)}, u32[]{:S(2)}) collective-permute-start(bf16[768,768]{0,1:T(8,128)(2,1)} %convolution_convert_fusion.3), channel_id=1, source_target_pairs={{0,16},{16,0},{1,17},{17,1},{2,18},{18,2},{3,19},{19,3},{4,20},{20... | collective-permute-start | bytes 3538952 | tf_op jit(solution)/shard_map/ppermute | solution.py:259
  331.8 54.3 %collective-permute-start.52 = (bf16[768,768]{0,1:T(8,128)(2,1)}, bf16[768,768]{0,1:T(8,128)(2,1)}, u32[]{:S(2)}, u32[]{:S(2)}) collective-permute-start(bf16[768,768]{0,1:T(8,128)(2,1)} %convolution_convert_fusion.2), channel_id=1, source_target_pairs={{0,2},{2,0},{1,3},{3,1},{4,6},{6,4},{5,7},{7,5},{8,10},{10,8},{9,1... | collective-permute-start | bytes 3538952 | tf_op jit(solution)/shard_map/ppermute | solution.py:259
  333.4 264.8 %reduce-scatter.12.cloned.1.call-start = ((), (), s32[]{:S(2)}) async-start(), calls=%async_computation.10 | async-start | bytes 2949120
  368.9 56.5 %collective-permute-start.54 = (bf16[768,384]{0,1:T(8,128)(2,1)}, bf16[768,384]{0,1:T(8,128)(2,1)}, u32[]{:S(2)}, u32[]{:S(2)}) collective-permute-start(bf16[768,384]{0,1:T(8,128)(2,1)} %convolution_convert_fusion.12), channel_id=1, source_target_pairs={{0,16},{16,0},{1,17},{17,1},{2,18},{18,2},{3,19},{19,3},{4,20},{20... | collective-permute-start | bytes 1769480 | tf_op jit(solution)/shard_map/ppermute | solution.py:259
  384.3 51.9 %collective-permute-start.48 = (bf16[768,384]{0,1:T(8,128)(2,1)}, bf16[768,384]{0,1:T(8,128)(2,1)}, u32[]{:S(2)}, u32[]{:S(2)}) collective-permute-start(bf16[768,384]{0,1:T(8,128)(2,1)} %pad_maximum_fusion.24), channel_id=1, source_target_pairs={{0,2},{2,0},{1,3},{3,1},{4,6},{6,4},{5,7},{7,5},{8,10},{10,8},{9,1... | collective-permute-start | bytes 1769480 | tf_op jit(solution)/shard_map/ppermute | solution.py:259
  398.6 201.1 %reduce-scatter.10.cloned.1.call-start = ((), (), s32[]{:S(2)}) async-start(), calls=%async_computation.9 | async-start | bytes 2211840
  398.6 30.9 %collective-permute-start.33 = (bf16[512,768]{1,0:T(8,128)(2,1)S(1)}, bf16[512,768]{1,0:T(8,128)(2,1)S(1)}, u32[]{:S(2)}, u32[]{:S(2)}) collective-permute-start(bf16[512,768]{1,0:T(8,128)(2,1)S(1)} %fusion.28), channel_id=1, source_target_pairs={{0,2},{2,0},{1,3},{3,1},{4,6},{6,4},{5,7},{7,5},{8,10},{10,8},{9,1... | collective-permute-start | bytes 2359304 | tf_op jit(solution)/shard_map/ppermute | solution.py:259
  423.7 30.2 %collective-permute-start.49 = (bf16[768,384]{0,1:T(8,128)(2,1)S(1)}, bf16[768,384]{0,1:T(8,128)(2,1)S(1)}, u32[]{:S(2)}, u32[]{:S(2)}) collective-permute-start(bf16[768,384]{0,1:T(8,128)(2,1)S(1)} %convolution_convert_fusion.13), channel_id=1, source_target_pairs={{0,16},{16,0},{1,17},{17,1},{2,18},{18,2},{3,19},{19,3},{4,20},{20... | collective-permute-start | bytes 1769480 | tf_op jit(solution)/shard_map/ppermute | solution.py:259
  461.3 197.6 %reduce-scatter.14.cloned.1.call-start = ((), (), s32[]{:S(2)}) async-start(), calls=%async_computation.11 | async-start | bytes 3686400 | tf_op jit(solution)/shard_map/reduce_scatter | solution.py:289
  466.7 54.3 %collective-permute-start.55 = (bf16[768,768]{0,1:T(8,128)(2,1)}, bf16[768,768]{0,1:T(8,128)(2,1)S(1)}, u32[]{:S(2)}, u32[]{:S(2)}) collective-permute-start(bf16[768,768]{0,1:T(8,128)(2,1)} %convolution_convert_fusion.1), channel_id=1, source_target_pairs={{0,16},{16,0},{1,17},{17,1},{2,18},{18,2},{3,19},{19,3},{4,20},{20... | collective-permute-start | bytes 3538952 | tf_op jit(solution)/shard_map/ppermute | solution.py:259
  470.2 53.8 %collective-permute-start.56 = (bf16[768,768]{0,1:T(8,128)(2,1)}, bf16[768,768]{0,1:T(8,128)(2,1)S(1)}, u32[]{:S(2)}, u32[]{:S(2)}) collective-permute-start(bf16[768,768]{0,1:T(8,128)(2,1)} %convolution_convert_fusion), channel_id=1, source_target_pairs={{0,2},{2,0},{1,3},{3,1},{4,6},{6,4},{5,7},{7,5},{8,10},{10,8},{9,1... | collective-permute-start | bytes 3538952 | tf_op jit(solution)/shard_map/ppermute | solution.py:259
  529.5 142.0 %all-gather.17.cloned.1.call-start = ((), (), s32[]{:S(2)}) async-start(), calls=%async_computation.8 | async-start | bytes 3538944 | tf_op jit(solution)/shard_map/all_gather | solution.py:592
  550.7 153.8 %all-gather.15.cloned.1.call-start = ((), (), s32[]{:S(2)}) async-start(), calls=%async_computation.7 | async-start | bytes 7077888 | tf_op jit(solution)/shard_map/all_gather | solution.py:592
  619.7 31.4 %collective-permute-start.53 = (bf16[192,2688]{1,0:T(8,128)(2,1)S(1)}, bf16[192,2688]{1,0:T(8,128)(2,1)S(1)}, u32[]{:S(2)}, u32[]{:S(2)}) collective-permute-start(bf16[192,2688]{1,0:T(8,128)(2,1)S(1)} %copy.141), channel_id=1, source_target_pairs={{0,18},{2,16},{1,19},{3,17},{4,22},{6,20},{5,23},{7,21},{8,26},{10... | collective-permute-start | bytes 3096584 | tf_op jit(solution)/shard_map/ppermute | solution.py:259
  659.0 30.9 %collective-permute-start.57 = (bf16[192,1920]{1,0:T(8,128)(2,1)}, bf16[192,1920]{1,0:T(8,128)(2,1)}, u32[]{:S(2)}, u32[]{:S(2)}) collective-permute-start(bf16[192,1920]{1,0:T(8,128)(2,1)} %reduce-scatter.14.cloned.1.call-done), channel_id=1, source_target_pairs={{16,2},{18,0},{17,3},{19,1},{20,6},{22,4},{21,7},{23,5},{24,10},{2... | collective-permute-start | bytes 2211848 | tf_op jit(solution)/shard_map/ppermute | solution.py:259
  (267 other events, 2893.5 us)
Sparse Core Ops, SparseCore 0:
  66.7 53.8 all-gather.6
  133.2 40.3 all-gather.8
  184.7 59.5 all-gather.10
  333.6 40.8 all-gather.12
  398.7 46.9 reduce-scatter.11
  461.5 36.5 reduce-scatter.9
  529.7 55.2 reduce-scatter.13
  587.4 36.5 all-gather.16
  625.8 65.0 all-gather.14

commit v3 on v2

--- a/solution.py
+++ b/solution.py
@@ -13,7 +13,8 @@
 MASKED = -1000000000.0
 BF = jnp.bfloat16
 F32 = jnp.float32
-BLOCK = 256
+FORWARD_BLOCK = 256
+BACKWARD_BLOCK = 512
 
 
 def dot(a, b, ca, cb):
@@ -21,20 +22,25 @@
 
 
 def fill_bias(mode, seg, place_ref, key_bias_ref, key_mark_ref, q_mark_ref, bias_ref):
-    lanes = bias_ref.shape[1]
+    lanes = FORWARD_BLOCK
+    pieces = bias_ref.shape[1] // lanes
     for at in range(0, bias_ref.shape[0], seg):
         keys = pl.ds(at, seg)
         key_bias = key_bias_ref[keys, :]
-        if mode == "all":
-            bias_ref[keys, :] = jnp.broadcast_to(key_bias, (seg, lanes))
-            continue
-        key_place = place_ref[at // seg] + lax.broadcasted_iota(jnp.int32, (seg, lanes), 0)
-        query_place = place_ref[4 + pl.program_id(0)] + lax.broadcasted_iota(jnp.int32, (seg, lanes), 1)
-        if mode == "causal":
-            allowed = key_place <= query_place
-        else:
-            allowed = (jnp.abs(key_place - query_place) <= WINDOW // 2) | (key_mark_ref[keys, :] + q_mark_ref[...] > 0.5)
-        bias_ref[keys, :] = jnp.where(allowed, key_bias, MASKED)
+        for piece in range(pieces):
+            queries = pl.ds(piece * lanes, lanes)
+            if mode == "all":
+                bias_ref[keys, queries] = jnp.broadcast_to(key_bias, (seg, lanes))
+                continue
+            key_place = place_ref[at // seg] + lax.broadcasted_iota(jnp.int32, (seg, lanes), 0)
+            first = place_ref[4 + pl.program_id(0) * pieces + piece]
+            query_place = first + lax.broadcasted_iota(jnp.int32, (seg, lanes), 1)
+            if mode == "causal":
+                allowed = key_place <= query_place
+            else:
+                marked = key_mark_ref[keys, :] + q_mark_ref[:, queries] > 0.5
+                allowed = (jnp.abs(key_place - query_place) <= WINDOW // 2) | marked
+            bias_ref[keys, queries] = jnp.where(allowed, key_bias, MASKED)
 
 
 def attend_forward_kernel(mode, chunks, place_ref, *refs):
@@ -79,11 +85,11 @@
             lse_ref[head : head + 1, :] = highest + jnp.log(summed)
 
 
-def mask_specs(half):
+def mask_specs(half, block):
     return [
         pl.BlockSpec((2 * half, 1), lambda b, p: (0, 0)),
         pl.BlockSpec((2 * half, 1), lambda b, p: (0, 0)),
-        pl.BlockSpec((1, BLOCK), lambda b, p: (0, b)),
+        pl.BlockSpec((1, block), lambda b, p: (0, b)),
     ]
 
 
@@ -93,22 +99,22 @@
     half = near[0].shape[1]
     heads = chunks * cut // HD
     side = pl.BlockSpec((2 * cut, half), lambda b, p: (0, 0))
-    lane = pl.BlockSpec((cut, BLOCK), lambda b, p: (0, b))
+    lane = pl.BlockSpec((cut, FORWARD_BLOCK), lambda b, p: (0, b))
     out = pl.pallas_call(
         functools.partial(attend_forward_kernel, mode, chunks),
         grid_spec=pltpu.PrefetchScalarGridSpec(
             num_scalar_prefetch=1,
-            grid=(rows // BLOCK,),
-            in_specs=[lane] * chunks + [side] * (2 * chunks) + mask_specs(half),
-            out_specs=[lane] * (2 * chunks) + [pl.BlockSpec((heads, BLOCK), lambda b, p: (0, b))],
-            scratch_shapes=[pltpu.VMEM((2 * half, BLOCK), F32)],
+            grid=(rows // FORWARD_BLOCK,),
+            in_specs=[lane] * chunks + [side] * (2 * chunks) + mask_specs(half, FORWARD_BLOCK),
+            out_specs=[lane] * (2 * chunks) + [pl.BlockSpec((heads, FORWARD_BLOCK), lambda b, p: (0, b))],
+            scratch_shapes=[pltpu.VMEM((2 * half, FORWARD_BLOCK), F32)],
         ),
         out_shape=[jax.ShapeDtypeStruct((cut, rows), BF)] * chunks
         + [jax.ShapeDtypeStruct((cut, rows), F32)] * chunks
         + [jax.ShapeDtypeStruct((heads, rows), F32)],
         compiler_params=pltpu.CompilerParams(vmem_limit_bytes=48 * 1024 * 1024),
         cost_estimate=pl.CostEstimate(
-            flops=32 * chunks * cut * rows * half, bytes_accessed=8 * chunks * cut * half, transcendentals=0
+            flops=cut * rows, bytes_accessed=cut * rows, transcendentals=0
         ),
     )(mask[0], *q, *near, *far, *mask[1:])
     return (out[:chunks], out[chunks : 2 * chunks], out[2 * chunks])
@@ -177,27 +183,27 @@
     half = near[0].shape[1]
     heads = chunks * cut // HD
     side = pl.BlockSpec((2 * cut, half), lambda b, p: (0, 0))
-    lane = pl.BlockSpec((cut, BLOCK), lambda b, p: (0, b))
+    lane = pl.BlockSpec((cut, BACKWARD_BLOCK), lambda b, p: (0, b))
     key_side = pl.BlockSpec((2 * half, 2 * cut), lambda b, p: (0, 0))
     out = pl.pallas_call(
         functools.partial(attend_backward_kernel, mode, chunks),
         grid_spec=pltpu.PrefetchScalarGridSpec(
             num_scalar_prefetch=1,
-            grid=(rows // BLOCK,),
+            grid=(rows // BACKWARD_BLOCK,),
             in_specs=[lane] * chunks
             + [side] * (2 * chunks)
-            + mask_specs(half)
+            + mask_specs(half, BACKWARD_BLOCK)
             + [lane] * chunks
-            + [pl.BlockSpec((heads, BLOCK), lambda b, p: (0, b))]
+            + [pl.BlockSpec((heads, BACKWARD_BLOCK), lambda b, p: (0, b))]
             + [lane] * chunks,
             out_specs=[lane] * chunks + [key_side] * chunks,
-            scratch_shapes=[pltpu.VMEM((2 * half, 2 * cut), F32)] * chunks + [pltpu.VMEM((2 * half, BLOCK), F32)],
+            scratch_shapes=[pltpu.VMEM((2 * half, 2 * cut), F32)] * chunks + [pltpu.VMEM((2 * half, BACKWARD_BLOCK), F32)],
         ),
         out_shape=[jax.ShapeDtypeStruct((cut, rows), BF)] * chunks
         + [jax.ShapeDtypeStruct((2 * half, 2 * cut), BF)] * chunks,
         compiler_params=pltpu.CompilerParams(vmem_limit_bytes=56 * 1024 * 1024),
         cost_estimate=pl.CostEstimate(
-            flops=80 * chunks * cut * rows * half, bytes_accessed=16 * chunks * cut * half, transcendentals=0
+            flops=cut * rows, bytes_accessed=cut * rows, transcendentals=0
         ),
     )(mask[0], *q, *near, *far, *mask[1:], *wide, lse, *grad)
     return (out[:chunks], out[chunks:])
@@ -365,8 +371,7 @@
     tgt_bias = jnp.where(tgt_place < tgt_length, 0.0, MASKED).astype(F32)[:, None]
 
     def places(place, queries):
-        size = place.shape[0] // 4
-        return jnp.concatenate([place[::size], queries[::BLOCK]])
+        return jnp.concatenate([place[:: place.shape[0] // 4], queries[::FORWARD_BLOCK]])
 
     src_chip = 2 * src_own
     tgt_chip = 2 * tgt_own
@@ -555,10 +560,11 @@
     back_one, dnorm_e1 = norm_back(back_two + back, enc_kept_one, norm_e[1])
     mixed_grad = chip(back_one.astype(BF))
     ctx_grad = project_back(mixed_grad, w_e["qp"], heads)
+    target_grad = (back_zero + target_mine + tie(target_other, back_one).astype(F32)).astype(BF)
+    ctx_grad[0] = tie(ctx_grad[0], target_grad)
     enc_dq, enc_dkv = attend_backward("window", enc_q, enc_near, enc_far, enc_mask, enc_wide, enc_lse, ctx_grad)
-    target_grad = (back_zero + target_mine + tie(target_other, enc_dq[0]).astype(F32)).astype(BF)
     normed_mine, normed_other, leaving = all_rows(w_e["kv"], enc_dkv, project(enc_dq, w_e["qp"], 0))
-    grad_qp_e = chip_total(two_sided(low_chip, enc_dq, mixed_grad, enc_ctx), False)
+    grad_qp_e = chip_total(two_sided(low_chip, enc_dq, mixed_grad, enc_ctx), True)
     grad_kv_e = chip_total(lambda r: dot(normed_low, enc_dkv[r], 0, 0), True)
 
     grad_up_d, grad_down_d = (grad_up_d(asking_grad[0]), grad_down_d(asking_grad[0]))
@@ -573,21 +579,22 @@
 
     dec_feed = cut_scatter([grad_up_d, grad_down_d], False)
     dec_rest = cut_scatter([grad_cross_d, grad_kv_d, grad_qp_d], False)
-    dec_sum = jnp.concatenate([dec_rest, dec_feed], axis=1)
-    dec_sum = dec_sum + crossing(dec_sum.astype(BF), 1).astype(F32)
+    feed_more = crossing(dec_feed.astype(BF), 1)
+    rest_more = crossing(dec_rest.astype(BF), 1)
+    dec_feed = dec_feed + feed_more.astype(F32)
+    dec_rest = dec_rest + rest_more.astype(F32)
     enc_feed = cut_scatter([grad_cross_e, grad_up_e, grad_down_e], False)
     enc_attn = cut_scatter([grad_kv_e, grad_qp_e], True)
     enc_feed = enc_feed + crossing(enc_feed.astype(BF), 0).astype(F32)
-    enc_attn = enc_attn + crossing(enc_attn.astype(BF), 0).astype(F32)
-    cross_width = sizes["cross"]
-    cross = jnp.where(section == 0, enc_feed[:, :cross_width], dec_sum[:, :cross_width])
-    attn = jnp.where(section == 0, enc_attn, dec_sum[:, cross_width : cross_width + attn_width])
-    feed = jnp.where(section == 0, enc_feed[:, cross_width:], dec_sum[:, cross_width + attn_width :])
     norm_sum = everywhere(
         jnp.stack([jnp.stack([dnorm_e0, dnorm_e1, dnorm_e2]), jnp.stack([dnorm_d0, dnorm_d1, dnorm_d2])])
     )
     norm_share = lax.dynamic_slice(norm_sum, (section, 0, 0, lax.axis_index("dp") * cut), (1, 3, 2, cut))
-
+    enc_attn = enc_attn + crossing(tie(enc_attn, norm_sum).astype(BF), 0).astype(F32)
+    cross_width = sizes["cross"]
+    cross = jnp.where(section == 0, enc_feed[:, :cross_width], dec_rest[:, :cross_width])
+    attn = jnp.where(section == 0, enc_attn, dec_rest[:, cross_width:])
+    feed = jnp.where(section == 0, enc_feed[:, cross_width:], dec_feed)
     def everyone(rows):
         full = lax.all_gather(rows, ("section", "ty", "tc"), tiled=True)
         return full.reshape(2, -1, width)

time: 734 us -> 720 us (0.981)
  matrix products: 143 us -> 126 us
  waiting for transfers between devices: 181 us -> 189 us
  starting transfers between devices: 66.1 us -> 73.8 us
    dot_general x84, matrix products: 143 us -> 126 us  [dot(): lax.dot_general(a, b, (((ca,), (cb,)), ((), ())), preferred_element_type=...]
    all_gather x3, waiting for transfers between devices: 0.01 us -> 11.4 us  [everyone(): full = lax.all_gather(rows, ('section', 'ty', 'tc'), tiled=True)]
    ppermute x63 -> x64, starting transfers between devices: 65.2 us -> 72.6 us  [hop(): return lax.ppermute(value, axis, pairs)]
    ppermute x63 -> x64, waiting for transfers between devices: 168 us -> 162 us  [hop(): return lax.ppermute(value, axis, pairs)]
    unnamed x454 -> x492, local copies, waits for them, and re-layouts: 49.4 us -> 46 us
  transfers between devices with their start and end apart: 72 -> 73, of which waited for: 29 -> 29; matrix products, arithmetic and copies ran while one was open for 38% -> 34% of each run, Pallas kernels for 16% -> 16%
where the time goes in v3:
time: 720 us; the launch traced here: 712 us
  waiting for transfers between devices  189 us (26%)
  matrix products  126 us (18%)
  Pallas kernels  124 us (17%)
  local copies, waits for them, and re-layouts  90.4 us (13%)
  starting transfers between devices  73.8 us (10%)
  other arithmetic  73.4 us (10%)
  between operations  34.1 us (5%)
    ppermute x64, waiting for transfers between devices, hop(): return lax.ppermute(value, axis, pairs)  162 us
    dot_general x84, matrix products, dot(): lax.dot_general(a, b, (((ca,), (cb,)), ((), ())), preferred_element_type=...  126 us
    pallas_call x3, Pallas kernels, attend_backward(): pl.pallas_call(functools.partial(attend_backward_kernel, mode, chunks), g...  74.8 us
    ppermute x64, starting transfers between devices, hop(): return lax.ppermute(value, axis, pairs)  72.6 us
    pallas_call x3, Pallas kernels, attend_forward(): pl.pallas_call(functools.partial(attend_forward_kernel, mode, chunks), gr...  49.2 us
    unnamed x492, local copies, waits for them, and re-layouts  46 us
  transfers between devices with their start and end apart: 73, of which 29 were waited for; matrix products, arithmetic and copies ran while one was open for 34% of the time, Pallas kernels for 16%

profile of v3, /device:TPU:0, one launch (start us, length us, event | category | flops | bytes accessed | tf_op | source)
XLA Modules:
  0.0 711.6 jit_solution(4318680440791005035)
XLA Ops:
  44.8 7.2 %collective-permute-done.10.refs_3_ = bf16[192,768]{1,0:T(8,128)(2,1)S(1)} collective-permute-done((bf16[192,768]{1,0:T(8,128)(2,1)S(1)}, bf16[192,768]{1,0:T(8,128)(2,1)S(1)}, u32[]{:S(2)}, u32[]{:S(2)}) %collective-permute-start.10) | collective-permute-done | bytes 294944 | tf_op jit(solution)/shard_map/ppermute | solution.py:265
  56.7 7.2 %fusion.164 = (bf16[2048,768]{1,0:T(8,128)(2,1)}, f32[2048,768]{1,0:T(8,128)}, f32[2048,768]{1,0:T(8,128)}) fusion(f32[768]{0:T(1024)S(1)} %get-tuple-element.144, f32[768]{0:T(1024)S(1)} %get-tuple-element.145, f32[2048]{0:T(1024)S(1)} %copy-done.176, f32[2048]{0:T(1024)S(1)} %copy-done.163, bf16[512,768]{1,0:T(8,128)(2,1)S(1)} %get-tuple-element.179, ...), kind=kLoop, calls=%fused_computation.433 | loop fusion | flops 20447232 | bytes 18896896 | tf_op jit(solution)/shard_map/convert_element_type | solution.py:489
  73.3 7.9 %collective-permute-done.12 = bf16[768,384]{1,0:T(8,128)(2,1)S(1)} collective-permute-done((bf16[768,384]{1,0:T(8,128)(2,1)S(1)}, bf16[768,384]{1,0:T(8,128)(2,1)S(1)}, u32[]{:S(2)}, u32[]{:S(2)}) %collective-permute-start.12) | collective-permute-done | bytes 589856 | tf_op jit(solution)/shard_map/ppermute | solution.py:265
  84.5 28.7 %shard_map.189 = (bf16[192,1024]{1,0:T(8,128)(2,1)S(1)}, bf16[192,1024]{1,0:T(8,128)(2,1)S(1)}, f32[192,1024]{1,0:T(8,128)S(1)}, f32[192,1024]{1,0:T(8,128)S(1)}, f32[6,1024]{1,0:T(8,128)S(1)}) custom-call(s32[8]{0:T(128)S(1)} %pad_add_fusion.7.place_ref, bf16[192,1024]{1,0:T(8,128)(2,1)S(1)} %fusion.37.refs_0_, bf16[192,1024]{1,0:T(8,128)(2,1)S(1)} %fusion.38.refs_1_, ...), custom_call_target="tpu_custom_call" | custom-call | flops 196608 | bytes 196608 | tf_op jit(solution)/shard_map/pallas_call | solution.py:103
  133.4 4.9 multiply_convert_fusion.3
  138.3 15.2 %collective-permute-done.16 = bf16[768,768]{1,0:T(8,128)(2,1)} collective-permute-done((bf16[768,768]{1,0:T(8,128)(2,1)}, bf16[768,768]{1,0:T(8,128)(2,1)}, u32[]{:S(2)}, u32[]{:S(2)}) %collective-permute-start.16) | collective-permute-done | bytes 1179680 | tf_op jit(solution)/shard_map/ppermute | solution.py:265
  153.5 4.9 multiply_convert_fusion.2
  185.5 13.9 %collective-permute-done.20 = bf16[512,768]{1,0:T(8,128)(2,1)S(1)} collective-permute-done((bf16[512,768]{1,0:T(8,128)(2,1)S(1)}, bf16[512,768]{1,0:T(8,128)(2,1)S(1)}, u32[]{:S(2)}, u32[]{:S(2)}) %collective-permute-start.20) | collective-permute-done | bytes 786464 | tf_op jit(solution)/shard_map/ppermute | solution.py:265
  200.3 10.5 %collective-permute-done.1 = bf16[768,384]{1,0:T(8,128)(2,1)S(1)} collective-permute-done((bf16[768,384]{1,0:T(8,128)(2,1)S(1)}, bf16[768,384]{1,0:T(8,128)(2,1)S(1)}, u32[]{:S(2)}, u32[]{:S(2)}) %collective-permute-start.1) | collective-permute-done | bytes 589856 | tf_op jit(solution)/shard_map/ppermute | solution.py:265
  212.3 7.7 %shard_map.187 = (bf16[192,512]{1,0:T(8,128)(2,1)S(1)}, bf16[192,512]{1,0:T(8,128)(2,1)S(1)}, f32[192,512]{1,0:T(8,128)S(1)}, f32[192,512]{1,0:T(8,128)S(1)}, f32[6,512]{1,0:T(8,128)S(1)}) custom-call(s32[6]{0:T(128)S(1)} %get-tuple-element.214.place_ref, bf16[192,512]{1,0:T(8,128)(2,1)S(1)} %fusion.43.refs_0_, bf16[192,512]{1,0:T(8,128)(2,1)S(1)} %fusion.44.refs_1_, ...), custom_call_target="tpu_custom_call" | custom-call | flops 98304 | bytes 98304 | tf_op jit(solution)/shard_map/pallas_call | solution.py:103
  225.7 14.0 %all-gather.11.cloned.1.call-done = bf16[768,1920]{1,0:T(8,128)(2,1)} async-done(((bf16[192,1920]{1,0:T(8,128)(2,1)}), bf16[768,1920]{1,0:T(8,128)(2,1)}) %all-gather.11.cloned.1.call-update) | async-done | bytes 2949136 | tf_op jit(solution)/shard_map/all_gather | solution.py:279
  248.7 7.3 %collective-permute-done.6 = bf16[768,384]{1,0:T(8,128)(2,1)S(1)} collective-permute-done((bf16[768,384]{1,0:T(8,128)(2,1)S(1)}, bf16[768,384]{1,0:T(8,128)(2,1)S(1)}, u32[]{:S(2)}, u32[]{:S(2)}) %collective-permute-start.6) | collective-permute-done | bytes 589856 | tf_op jit(solution)/shard_map/ppermute | solution.py:265
  257.8 12.8 %shard_map.190 = (bf16[192,512]{1,0:T(8,128)(2,1)S(1)}, bf16[192,512]{1,0:T(8,128)(2,1)S(1)}, f32[192,512]{1,0:T(8,128)S(1)}, f32[192,512]{1,0:T(8,128)S(1)}, f32[6,512]{1,0:T(8,128)S(1)}) custom-call(s32[6]{0:T(128)S(1)} %get-tuple-element.215.place_ref, bf16[192,512]{1,0:T(8,128)(2,1)S(1)} %fusion.45.refs_0_, bf16[192,512]{1,0:T(8,128)(2,1)S(1)} %fusion.46.refs_1_, ...), custom_call_target="tpu_custom_call" | custom-call | flops 98304 | bytes 98304 | tf_op jit(solution)/shard_map/pallas_call | solution.py:103
  277.2 23.4 %collective-permute-done.24 = bf16[768,768]{1,0:T(8,128)(2,1)S(1)} collective-permute-done((bf16[768,768]{1,0:T(8,128)(2,1)S(1)}, bf16[768,768]{1,0:T(8,128)(2,1)S(1)}, u32[]{:S(2)}, u32[]{:S(2)}) %collective-permute-start.24) | collective-permute-done | bytes 1179680 | tf_op jit(solution)/shard_map/ppermute | solution.py:265
  331.3 21.1 %shard_map.191 = (bf16[192,512]{1,0:T(8,128)(2,1)}, bf16[192,512]{1,0:T(8,128)(2,1)}, bf16[2048,384]{1,0:T(8,128)(2,1)}, bf16[2048,384]{1,0:T(8,128)(2,1)}) custom-call(s32[6]{0:T(128)} %copy-done.43, bf16[192,512]{1,0:T(8,128)(2,1)} %copy-done.17, bf16[192,512]{1,0:T(8,128)(2,1)} %copy-done.18, bf16[384,1024]{1,0:T(8,128)(2,1)} %copy-done.3, ...), custom_call_target="tpu_custom_call" | custom-call | flops 98304 | bytes 98304 | tf_op jit(solution)/shard_map/pallas_call | solution.py:188
  393.6 12.0 %shard_map.192 = (bf16[192,512]{1,0:T(8,128)(2,1)}, bf16[192,512]{1,0:T(8,128)(2,1)}, bf16[1024,384]{1,0:T(8,128)(2,1)}, bf16[1024,384]{1,0:T(8,128)(2,1)}) custom-call(s32[6]{0:T(128)} %copy-done.42, bf16[192,512]{1,0:T(8,128)(2,1)} %copy-done.19, bf16[192,512]{1,0:T(8,128)(2,1)} %copy-done.20, bf16[384,512]{1,0:T(8,128)(2,1)} %copy-done.9, ...), custom_call_target="tpu_custom_call" | custom-call | flops 98304 | bytes 98304 | tf_op jit(solution)/shard_map/pallas_call | solution.py:188
  421.8 5.7 collective-permute-done.55
  461.9 7.1 %collective-permute-done.57 = bf16[768,384]{0,1:T(8,128)(2,1)S(1)} collective-permute-done((bf16[768,384]{0,1:T(8,128)(2,1)S(1)}, bf16[768,384]{0,1:T(8,128)(2,1)S(1)}, u32[]{:S(2)}, u32[]{:S(2)}) %collective-permute-start.57) | collective-permute-done | bytes 589856 | tf_op jit(solution)/shard_map/ppermute | solution.py:265
  484.6 41.7 %shard_map.193 = (bf16[192,1024]{1,0:T(8,128)(2,1)}, bf16[192,1024]{1,0:T(8,128)(2,1)}, bf16[2048,384]{1,0:T(8,128)(2,1)}, bf16[2048,384]{1,0:T(8,128)(2,1)}) custom-call(s32[8]{0:T(128)} %copy-done.44, bf16[192,1024]{1,0:T(8,128)(2,1)} %copy-done.13, bf16[192,1024]{1,0:T(8,128)(2,1)} %copy-done.14, bf16[384,1024]{1,0:T(8,128)(2,1)} %copy-done.7, ...), custom_call_target="tpu_custom_call" | custom-call | flops 196608 | bytes 196608 | tf_op jit(solution)/shard_map/pallas_call | solution.py:188
  556.2 8.7 %collective-permute-done.40 = bf16[768,384]{0,1:T(8,128)(2,1)S(1)} collective-permute-done((bf16[768,384]{0,1:T(8,128)(2,1)S(1)}, bf16[768,384]{0,1:T(8,128)(2,1)S(1)}, u32[]{:S(2)}, u32[]{:S(2)}) %collective-permute-start.40) | collective-permute-done | bytes 589856 | tf_op jit(solution)/shard_map/ppermute | solution.py:265
  614.5 7.9 %collective-permute-start.49 = (f32[2,3,2,768]{3,2,1,0:T(2,128)S(1)}, f32[2,3,2,768]{3,2,1,0:T(2,128)S(1)}, u32[]{:S(2)}, u32[]{:S(2)}) collective-permute-start(f32[2,3,2,768]{3,2,1,0:T(2,128)S(1)} %fusion.251), channel_id=1, source_target_pairs={{0,16},{16,0},{1,17},{17,1},{2,18},{18,2},{3,19},{19,3},{4,20},{20... | collective-permute-start | bytes 110600 | tf_op jit(solution)/shard_map/ppermute | solution.py:265
  643.1 11.6 %collective-permute-done.52 = bf16[192,768]{0,1:T(8,128)(2,1)} collective-permute-done((bf16[192,768]{0,1:T(8,128)(2,1)}, bf16[192,768]{0,1:T(8,128)(2,1)}, u32[]{:S(2)}, u32[]{:S(2)}) %collective-permute-start.52) | collective-permute-done | bytes 294944 | tf_op jit(solution)/shard_map/ppermute | solution.py:265
  659.2 12.1 %collective-permute-done.60 = bf16[192,1920]{1,0:T(8,128)(2,1)} collective-permute-done((bf16[192,1920]{1,0:T(8,128)(2,1)}, bf16[192,1920]{1,0:T(8,128)(2,1)}, u32[]{:S(2)}, u32[]{:S(2)}) %collective-permute-start.60) | collective-permute-done | bytes 737312 | tf_op jit(solution)/shard_map/ppermute | solution.py:265
  682.8 11.4 %all-gather.15.cloned.1.call-done = bf16[4096,768]{1,0:T(8,128)(2,1)} async-done(((bf16[512,768]{1,0:T(8,128)(2,1)}), bf16[4096,768]{1,0:T(8,128)(2,1)}) %all-gather.15.cloned.1.call-update) | async-done | bytes 6291472 | tf_op jit(solution)/shard_map/all_gather | solution.py:599
  (920 shorter events, 372.7 us)
Async XLA Ops:
  7.2 114.6 %all-gather.7.cloned.1.call-start = ((), (), s32[]{:S(2)}) async-start(), calls=%async_computation.3 | async-start | bytes 2949120 | tf_op jit(solution)/shard_map/all_gather | solution.py:279
  64.8 109.8 %all-gather.9.cloned.1.call-start = ((), (), s32[]{:S(2)}) async-start(), calls=%async_computation.4 | async-start | bytes 2211840 | tf_op jit(solution)/shard_map/all_gather | solution.py:279
  125.1 28.5 %collective-permute-start.16 = (bf16[768,768]{1,0:T(8,128)(2,1)}, bf16[768,768]{1,0:T(8,128)(2,1)}, u32[]{:S(2)}, u32[]{:S(2)}) collective-permute-start(bf16[768,768]{1,0:T(8,128)(2,1)} %get-tuple-element.191), channel_id=1, source_target_pairs={{0,16},{16,0},{1,17},{17,1},{2,18},{18,2},{3,19},{19,3},{4,20},{20... | collective-permute-start | bytes 3538952 | tf_op jit(solution)/shard_map/ppermute | solution.py:265
  126.7 31.7 %collective-permute-start.17 = (bf16[768,768]{1,0:T(8,128)(2,1)}, bf16[768,768]{1,0:T(8,128)(2,1)}, u32[]{:S(2)}, u32[]{:S(2)}) collective-permute-start(bf16[768,768]{1,0:T(8,128)(2,1)} %get-tuple-element.190), channel_id=1, source_target_pairs={{0,2},{2,0},{1,3},{3,1},{4,6},{6,4},{5,7},{7,5},{8,10},{10,8},{9,1... | collective-permute-start | bytes 3538952 | tf_op jit(solution)/shard_map/ppermute | solution.py:265
  133.4 106.4 %all-gather.11.cloned.1.call-start = ((), (), s32[]{:S(2)}) async-start(), calls=%async_computation.5 | async-start | bytes 3686400 | tf_op jit(solution)/shard_map/all_gather | solution.py:279
  178.2 408.9 %reduce-scatter.14.cloned.1.call-start = ((), (), s32[]{:S(2)}) async-start(), calls=%async_computation.11 | async-start | bytes 2949120 | tf_op jit(solution)/shard_map/reduce_scatter | solution.py:295
  180.8 40.6 %collective-permute-start.7 = (bf16[768,384]{1,0:T(8,128)(2,1)S(1)}, bf16[768,384]{1,0:T(8,128)(2,1)S(1)}, u32[]{:S(2)}, u32[]{:S(2)}) collective-permute-start(bf16[768,384]{1,0:T(8,128)(2,1)S(1)} %get-tuple-element.194), channel_id=1, source_target_pairs={{0,16},{16,0},{1,17},{17,1},{2,18},{18,2},{3,19},{19,3},{4,20},{20... | collective-permute-start | bytes 1769480 | tf_op jit(solution)/shard_map/ppermute | solution.py:265
  182.4 28.3 %collective-permute-start.1 = (bf16[768,384]{1,0:T(8,128)(2,1)S(1)}, bf16[768,384]{1,0:T(8,128)(2,1)S(1)}, u32[]{:S(2)}, u32[]{:S(2)}) collective-permute-start(bf16[768,384]{1,0:T(8,128)(2,1)S(1)} %get-tuple-element.196), channel_id=1, source_target_pairs={{0,2},{2,0},{1,3},{3,1},{4,6},{6,4},{5,7},{7,5},{8,10},{10,8},{9,1... | collective-permute-start | bytes 1769480 | tf_op jit(solution)/shard_map/ppermute | solution.py:265
  272.1 28.4 %collective-permute-start.24 = (bf16[768,768]{1,0:T(8,128)(2,1)S(1)}, bf16[768,768]{1,0:T(8,128)(2,1)S(1)}, u32[]{:S(2)}, u32[]{:S(2)}) collective-permute-start(bf16[768,768]{1,0:T(8,128)(2,1)S(1)} %get-tuple-element.189), channel_id=1, source_target_pairs={{0,16},{16,0},{1,17},{17,1},{2,18},{18,2},{3,19},{19,3},{4,20},{20... | collective-permute-start | bytes 3538952 | tf_op jit(solution)/shard_map/ppermute | solution.py:265
  274.8 28.2 %collective-permute-start.25 = (bf16[768,768]{1,0:T(8,128)(2,1)S(1)}, bf16[768,768]{1,0:T(8,128)(2,1)S(1)}, u32[]{:S(2)}, u32[]{:S(2)}) collective-permute-start(bf16[768,768]{1,0:T(8,128)(2,1)S(1)} %get-tuple-element.188), channel_id=1, source_target_pairs={{0,2},{2,0},{1,3},{3,1},{4,6},{6,4},{5,7},{7,5},{8,10},{10,8},{9,1... | collective-permute-start | bytes 3538952 | tf_op jit(solution)/shard_map/ppermute | solution.py:265
  323.6 45.8 %collective-permute-start.61 = (bf16[768,768]{0,1:T(8,128)(2,1)}, bf16[768,768]{0,1:T(8,128)(2,1)}, u32[]{:S(2)}, u32[]{:S(2)}) collective-permute-start(bf16[768,768]{0,1:T(8,128)(2,1)} %convolution_convert_fusion.1), channel_id=1, source_target_pairs={{0,16},{16,0},{1,17},{17,1},{2,18},{18,2},{3,19},{19,3},{4,20},{20... | collective-permute-start | bytes 3538952 | tf_op jit(solution)/shard_map/ppermute | solution.py:265
  327.1 44.6 %collective-permute-start.62 = (bf16[768,768]{0,1:T(8,128)(2,1)}, bf16[768,768]{0,1:T(8,128)(2,1)}, u32[]{:S(2)}, u32[]{:S(2)}) collective-permute-start(bf16[768,768]{0,1:T(8,128)(2,1)} %convolution_convert_fusion), channel_id=1, source_target_pairs={{0,2},{2,0},{1,3},{3,1},{4,6},{6,4},{5,7},{7,5},{8,10},{10,8},{9,1... | collective-permute-start | bytes 3538952 | tf_op jit(solution)/shard_map/ppermute | solution.py:265
  368.9 44.6 %collective-permute-start.53 = (bf16[768,384]{0,1:T(8,128)(2,1)}, bf16[768,384]{0,1:T(8,128)(2,1)}, u32[]{:S(2)}, u32[]{:S(2)}) collective-permute-start(bf16[768,384]{0,1:T(8,128)(2,1)} %pad_maximum_fusion.23), channel_id=1, source_target_pairs={{0,2},{2,0},{1,3},{3,1},{4,6},{6,4},{5,7},{7,5},{8,10},{10,8},{9,1... | collective-permute-start | bytes 1769480 | tf_op jit(solution)/shard_map/ppermute | solution.py:265
  376.5 214.5 %reduce-scatter.10.cloned.1.call-start = ((), (), s32[]{:S(2)}) async-start(), calls=%async_computation.9 | async-start | bytes 2211840 | tf_op jit(solution)/shard_map/reduce_scatter | solution.py:295
  430.9 202.5 %all-gather.13.cloned.1.call-start = ((), (), s32[]{:S(2)}) async-start(), calls=%async_computation.6 | async-start | bytes 3538944 | tf_op jit(solution)/shard_map/all_gather | solution.py:599
  431.5 208.9 %reduce-scatter.12.cloned.1.call-start = ((), (), s32[]{:S(2)}) async-start(), calls=%async_computation.10 | async-start | bytes 3686400 | tf_op jit(solution)/shard_map/reduce_scatter | solution.py:295
  458.9 69.9 %collective-permute-start.58 = (bf16[768,768]{0,1:T(8,128)(2,1)}, bf16[768,768]{0,1:T(8,128)(2,1)}, u32[]{:S(2)}, u32[]{:S(2)}) collective-permute-start(bf16[768,768]{0,1:T(8,128)(2,1)} %convolution_convert_fusion.3), channel_id=1, source_target_pairs={{0,16},{16,0},{1,17},{17,1},{2,18},{18,2},{3,19},{19,3},{4,20},{20... | collective-permute-start | bytes 3538952 | tf_op jit(solution)/shard_map/ppermute | solution.py:265
  474.3 57.9 %collective-permute-start.59 = (bf16[768,768]{0,1:T(8,128)(2,1)}, bf16[768,768]{0,1:T(8,128)(2,1)}, u32[]{:S(2)}, u32[]{:S(2)}) collective-permute-start(bf16[768,768]{0,1:T(8,128)(2,1)} %convolution_convert_fusion.2), channel_id=1, source_target_pairs={{0,2},{2,0},{1,3},{3,1},{4,6},{6,4},{5,7},{7,5},{8,10},{10,8},{9,1... | collective-permute-start | bytes 3538952 | tf_op jit(solution)/shard_map/ppermute | solution.py:265
  539.1 118.7 %all-gather.17.cloned.1.call-start = ((), (), s32[]{:S(2)}) async-start(), calls=%async_computation.8 | async-start | bytes 3538944 | tf_op jit(solution)/shard_map/all_gather | solution.py:599
  539.9 154.3 %all-gather.15.cloned.1.call-start = ((), (), s32[]{:S(2)}) async-start(), calls=%async_computation.7 | async-start | bytes 7077888 | tf_op jit(solution)/shard_map/all_gather | solution.py:599
  587.0 47.4 %collective-permute-start.63 = (bf16[192,1536]{1,0:T(8,128)(2,1)}, bf16[192,1536]{1,0:T(8,128)(2,1)S(1)}, u32[]{:S(2)}, u32[]{:S(2)}) collective-permute-start(bf16[192,1536]{1,0:T(8,128)(2,1)} %reduce-scatter.14.cloned.1.call-done), channel_id=1, source_target_pairs={{0,18},{2,16},{1,19},{3,17},{4,22},{6,20},{5,23},{7,21},{8,26},{10... | collective-permute-start | bytes 1769480 | tf_op jit(solution)/shard_map/ppermute | solution.py:265
  591.0 44.9 %collective-permute-start.56 = (bf16[192,1152]{1,0:T(8,128)(2,1)}, bf16[192,1152]{1,0:T(8,128)(2,1)S(1)}, u32[]{:S(2)}, u32[]{:S(2)}) collective-permute-start(bf16[192,1152]{1,0:T(8,128)(2,1)} %reduce-scatter.10.cloned.1.call-done), channel_id=1, source_target_pairs={{0,18},{2,16},{1,19},{3,17},{4,22},{6,20},{5,23},{7,21},{8,26},{10... | collective-permute-start | bytes 1327112 | tf_op jit(solution)/shard_map/ppermute | solution.py:265
  606.7 31.3 %collective-permute-start.44 = (bf16[192,768]{0,1:T(8,128)(2,1)}, bf16[192,768]{0,1:T(8,128)(2,1)S(1)}, u32[]{:S(2)}, u32[]{:S(2)}) collective-permute-start(bf16[192,768]{0,1:T(8,128)(2,1)} %add_convert_fusion.7), channel_id=1, source_target_pairs={{0,4},{4,8},{8,12},{12,0},{1,5},{5,9},{9,13},{13,1},{2,6},{6,10},{... | collective-permute-start | bytes 884744 | tf_op jit(solution)/shard_map/ppermute | solution.py:265
  640.4 30.9 %collective-permute-start.60 = (bf16[192,1920]{1,0:T(8,128)(2,1)}, bf16[192,1920]{1,0:T(8,128)(2,1)}, u32[]{:S(2)}, u32[]{:S(2)}) collective-permute-start(bf16[192,1920]{1,0:T(8,128)(2,1)} %reduce-scatter.12.cloned.1.call-done), channel_id=1, source_target_pairs={{16,2},{18,0},{17,3},{19,1},{20,6},{22,4},{21,7},{23,5},{24,10},{2... | collective-permute-start | bytes 2211848 | tf_op jit(solution)/shard_map/ppermute | solution.py:265
  (287 other events, 2830.2 us)
Sparse Core Ops, SparseCore 0:
  64.9 53.7 all-gather.6
  133.5 39.4 all-gather.8
  178.3 61.4 all-gather.10
  376.6 45.9 reduce-scatter.13
  431.0 35.6 reduce-scatter.9
  468.6 43.4 all-gather.12
  539.3 55.6 reduce-scatter.11
  596.9 43.3 all-gather.16
  642.2 51.8 all-gather.14
